TPU v7x, 32 devices: a whole 2x2x4 slice. The times are simulated.
32 devices in a mesh: dp: 8 (over z, x), tensor: 4 (over y, core).
Axes of the slice: x: 2, y: 2, z: 4, core: 2. Of those that a mesh axis runs over, the one named last changes fastest.
Arguments:
- activations: bfloat16 [4096, 4096], P('dp', 'tensor'), may hold values from -6 to 6
- base_weight: bfloat16 [4096, 4096], P('tensor'), may hold values from -8.4375 to 8.4375
- adapter_in: float32 [4096, 64], P('tensor'), may hold values from -0.09375 to 0.09375
- adapter_out: float32 [64, 4096], replicated, may hold values from -0.75 to 0.75
- magnitude: float32 [4096], replicated, may hold values from 0.5 to 2
- cotangent: bfloat16 [4096, 4096], P(('dp', 'tensor')), may hold values from -1.5 to 1.5
Outputs:
- output: bfloat16 [4096, 4096], P(('dp', 'tensor'))
- grad_act: bfloat16 [4096, 4096], P('dp', 'tensor')
- grad_in: float32 [4096, 64], P('tensor')
- grad_out: float32 [64, 4096], replicated
- grad_mag: float32 [4096], replicated
All inputs are finite; a program needn't handle non-finite values.
Results may differ from a plain program's by a relative error of at most 0.0057.
Values may be sent and summed in bfloat16 or wider, within the bound.
A program may use at most 128 MiB of HBM per device.

v0:
```python
import jax
import jax.numpy as jnp
from jax import lax
from jax.sharding import PartitionSpec as P

epsilon = 1e-06


def shards(activations, base_weight, adapter_in, adapter_out, magnitude, cotangent):
    highest = lax.Precision.HIGHEST
    lowrank = jnp.dot(adapter_in, adapter_out, precision=highest)
    merged = base_weight.astype(jnp.float32) + lowrank
    squares = jnp.sum(merged * merged, axis=0)
    square_sum = lax.psum(squares, "tensor")
    col_norm = jnp.sqrt(square_sum + epsilon)
    col_scale = magnitude / col_norm
    merged_low = merged.astype(jnp.bfloat16)
    act_rows = activations
    summed = lax.psum_scatter(
        jnp.dot(act_rows, merged_low, preferred_element_type=jnp.float32),
        "tensor",
        scatter_dimension=0,
        tiled=True,
    )
    output = (summed * col_scale).astype(jnp.bfloat16)
    cot_float = cotangent.astype(jnp.float32)
    grad_scaled = (cot_float * col_scale).astype(jnp.bfloat16)
    mag_slope = jnp.sum(cot_float * summed, axis=0) / col_norm
    block_part = lax.all_gather(grad_scaled, "tensor", axis=0, tiled=True)
    act_rows = activations
    product = lax.dot_general(
        block_part, merged_low, (((1,), (1,)), ((), ())), preferred_element_type=jnp.float32
    )
    act_total = product
    dir_total = lax.dot_general(
        act_rows, block_part, (((0,), (0,)), ((), ())), preferred_element_type=jnp.float32
    )
    act_total, grad_dir = (act_total, dir_total)
    grad_act = act_total.astype(jnp.bfloat16)
    slope_replica = lax.psum(mag_slope, "tensor")
    norm_coeff = -slope_replica * magnitude / (col_norm * col_norm)
    full_dir = grad_dir + merged * norm_coeff
    in_replica = jnp.dot(full_dir, adapter_out.T, precision=highest)
    cross_term = jnp.dot(adapter_in.T, full_dir, precision=highest)
    out_replica = lax.psum(cross_term, "tensor")
    grad_in, grad_out, grad_mag = lax.psum((in_replica, out_replica, slope_replica), "dp")
    return (output, grad_act, grad_in, grad_out, grad_mag)


def solution(mesh):
    in_specs = (
        P("dp", "tensor"),
        P("tensor", None),
        P("tensor", None),
        P(),
        P(),
        P(("dp", "tensor"), None),
    )
    out_specs = (P(("dp", "tensor"), None), P("dp", "tensor"), P("tensor", None), P(), P())
    return jax.shard_map(shards, mesh=mesh, in_specs=in_specs, out_specs=out_specs, check_vma=False)
```

profile of v0, /device:TPU:25, one launch (start us, length us, event | category | flops | bytes accessed | tf_op | source)
XLA Modules:
  0.0 322.0 jit_solution(6677763606578367983)
XLA Ops:
  7.2 0.0 reduce-scatter.2.cloned.1.call-start
  7.2 17.7 %multiply_reduce_fusion = (f32[4096]{0:T(1024)S(1)}, f32[1024,4096]{1,0:T(8,128)S(1)}) fusion(f32[1024,64]{0,1:T(8,128)} %param.8, f32[64,4096]{1,0:T(8,128)} %param.9, bf16[1024,4096]{1,0:T(8,128)(2,1)} %param.7), kind=kOutput, calls=%fused_computation.1 | convolution fusion | flops 3237998592 | bytes 26492928 | tf_op jit(solution)/shard_map/dot_general | solution.py:11
  25.0 5.7 %copy-done.2 = f32[1024,4096]{1,0:T(8,128)} copy-done((f32[1024,4096]{1,0:T(8,128)}, f32[1024,4096]{1,0:T(8,128)S(1)}, u32[]{:S(2)}) %copy-start.2) | copy-done | bytes 16777240
  30.7 7.0 %convolution_bitcast_fusion = f32[512,4096]{0,1:T(8,128)} fusion(bf16[512,1024]{1,0:T(8,128)(2,1)S(1)} %copy-done, f32[1024,4096]{1,0:T(8,128)S(1)} %get-tuple-element.16), kind=kOutput, calls=%fused_computation.3 | convolution fusion | flops 4299161600 | bytes 26214400 | tf_op jit(solution)/shard_map/dot_general | solution.py:20
  37.7 0.0 all-gather.2.cloned.1.call-start
  37.8 1.1 copy-done.5
  38.9 0.7 copy.11
  39.6 9.7 %psum.42 = f32[4096]{0:T(1024)S(1)} all-reduce(f32[4096]{0:T(1024)S(1)} %get-tuple-element.15), channel_id=1, replica_groups=mesh['dp'=8,'tensor'=4] {'tensor'}, use_global_device_ids=true, to_apply=%region_2.0 | all-reduce | flops 4096 | bytes 32768 | tf_op jit(solution)/shard_map/psum | solution.py:14
  49.3 61.3 %reduce-scatter.2.cloned.1.call-done = f32[128,4096]{0,1:T(8,128)} async-done(((f32[512,4096]{0,1:T(8,128)}), f32[128,4096]{0,1:T(8,128)}) %reduce-scatter.2.cloned.1.call-update) | async-done | bytes 2097168 | tf_op jit(solution)/shard_map/reduce_scatter | solution.py:19
  110.6 3.3 %fusion.4 = (f32[4096]{0:T(1024)S(1)}, bf16[128,4096]{0,1:T(8,128)(2,1)S(1)}, bf16[128,4096]{0,1:T(8,128)(2,1)}) fusion(f32[128,4096]{0,1:T(8,128)} %reduce-scatter.2.cloned.1.call-done, bf16[128,4096]{0,1:T(8,128)(2,1)S(1)} %copy.11, f32[4096]{0:T(1024)S(1)} %fusion.9), kind=kLoop, calls=%fused_computation.11 | loop fusion | flops 3665920 | bytes 5275648 | tf_op jit(solution)/shard_map/reduce_sum | solution.py:28
  113.9 0.0 all-reduce.4.cloned.1.call-start
  113.9 1.3 copy.13
  115.3 9.7 %psum.43 = f32[4096]{0:T(1024)S(1)} all-reduce(f32[4096]{0:T(1024)S(1)} %fusion.8), channel_id=1, replica_groups=mesh['dp'=8,'tensor'=4] {'tensor'}, use_global_device_ids=true, to_apply=%region_4.0 | all-reduce | flops 4096 | bytes 32768 | tf_op jit(solution)/shard_map/psum | solution.py:40
  125.0 26.5 %psum.47 = f32[4096]{0:T(1024)} all-reduce(f32[4096]{0:T(1024)S(1)} %psum.43), channel_id=1, replica_groups=mesh['dp'=8,'tensor'=4] {'dp'}, use_global_device_ids=true, to_apply=%region_8.0 | all-reduce | flops 4096 | bytes 32768 | tf_op jit(solution)/shard_map/psum | solution.py:46
  151.5 0.0 all-gather.2.cloned.1.call-done
  151.5 12.7 %bitcast_add_fusion = f32[1024,4096]{1,0:T(8,128)} fusion(f32[1024,4096]{1,0:T(8,128)} %copy-done.2, bf16[512,4096]{0,1:T(8,128)(2,1)} %all-gather.2.cloned.1.call-done, bf16[512,1024]{1,0:T(8,128)(2,1)S(1)} %copy-done, f32[4096]{0:T(1024)S(1)} %multiply_divide_fusion), kind=kOutput, calls=%fused_computation | convolution fusion | flops 4303355904 | bytes 38813696 | tf_op jit(solution)/shard_map/dot_general | solution.py:35
  164.3 15.5 %convolution_bitcast_fusion.1 = f32[64,4096]{1,0:T(8,128)} fusion(f32[1024,4096]{1,0:T(8,128)} %bitcast_add_fusion, f32[1024,64]{0,1:T(8,128)S(1)} %copy-done.4), kind=kOutput, calls=%fused_computation.4 | convolution fusion | flops 3221225472 | bytes 18087936 | tf_op jit(solution)/shard_map/dot_general | solution.py:44
  179.8 0.3 all-reduce.6.cloned.1.call-start
  180.1 20.4 %fusion.10 = f32[1024,64]{0,1:T(8,128)} fusion(f32[1024,4096]{1,0:T(8,128)} %bitcast_add_fusion, f32[64,4096]{1,0:T(8,128)S(1)} %copy-done.3), kind=kOutput, calls=%fused_computation.18 | convolution fusion | flops 3221225472 | bytes 18087936 | tf_op jit(solution)/shard_map/dot_general | solution.py:43
  200.6 24.1 %all-reduce.4.cloned.1.call-done = f32[64,4096]{1,0:T(8,128)} async-done(((f32[64,4096]{1,0:T(8,128)}), f32[64,4096]{1,0:T(8,128)}) %all-reduce.4.cloned.1.call-update) | async-done | bytes 1048592 | tf_op jit(solution)/shard_map/psum | solution.py:45
  224.7 12.6 %fusion.5 = bf16[512,1024]{1,0:T(8,128)(2,1)} fusion(bf16[512,4096]{0,1:T(8,128)(2,1)} %all-gather.2.cloned.1.call-done, f32[1024,4096]{1,0:T(8,128)} %copy-done.2), kind=kOutput, calls=%fused_computation.13 | convolution fusion | flops 4299685888 | bytes 22020096 | tf_op jit(solution)/shard_map/dot_general | solution.py:31
  237.3 74.2 %all-reduce.6.cloned.1.call-done = (f32[1024,64]{0,1:T(8,128)}, f32[64,4096]{1,0:T(8,128)}) async-done(((f32[1024,64]{0,1:T(8,128)}, f32[64,4096]{1,0:T(8,128)}), (f32[1024,64]{0,1:T(8,128)}, f32[64,4096]{1,0:T(8,128)})) %all-reduce.6.cloned.1.call-update) | async-done | bytes 1310736 | tf_op jit(solution)/shard_map/psum | solution.py:46
  311.5 1.7 copy.18
  313.2 2.3 copy.19
  (19 shorter events, 0.1 us)
Async XLA Ops:
  7.2 23.5 %copy-start = (bf16[512,1024]{1,0:T(8,128)(2,1)S(1)}, bf16[512,1024]{1,0:T(8,128)(2,1)}, u32[]{:S(2)}) copy-start(bf16[512,1024]{1,0:T(8,128)(2,1)} %param.6) | copy-start | bytes 3145732
  7.2 103.4 %reduce-scatter.2.cloned.1.call-start = ((), (), s32[]{:S(2)}) async-start(), calls=%async_computation.1 | async-start | bytes 10485760 | tf_op jit(solution)/shard_map/reduce_scatter | solution.py:19
  25.0 5.7 %copy-start.2 = (f32[1024,4096]{1,0:T(8,128)}, f32[1024,4096]{1,0:T(8,128)S(1)}, u32[]{:S(2)}) copy-start(f32[1024,4096]{1,0:T(8,128)S(1)} %get-tuple-element.16) | copy-start | bytes 50331652
  37.7 1.2 copy-start.5
  37.7 11.6 %copy-start.6 = (f32[4096]{0:T(1024)S(1)}, f32[4096]{0:T(1024)}, u32[]{:S(2)}) copy-start(f32[4096]{0:T(1024)} %param.10) | copy-start | bytes 49156
  37.7 113.8 %all-gather.2.cloned.1.call-start = ((), (), s32[]{:S(2)}) async-start(), calls=%async_computation.2 | async-start | bytes 5242880 | tf_op jit(solution)/shard_map/all_gather | solution.py:29
  113.9 110.8 %all-reduce.4.cloned.1.call-start = ((), (), s32[]{:S(2)}) async-start(), calls=%async_computation.3 | async-start | bytes 2097152 | tf_op jit(solution)/shard_map/psum | solution.py:45
  151.5 12.8 %copy-start.4 = (f32[1024,64]{0,1:T(8,128)S(1)}, f32[1024,64]{0,1:T(8,128)}, u32[]{:S(2)}) copy-start(f32[1024,64]{0,1:T(8,128)} %param.8) | copy-start | bytes 786436
  164.3 15.8 %copy-start.3 = (f32[64,4096]{1,0:T(8,128)S(1)}, f32[64,4096]{1,0:T(8,128)}, u32[]{:S(2)}) copy-start(f32[64,4096]{1,0:T(8,128)} %param.9) | copy-start | bytes 3145732
  179.8 131.7 %all-reduce.6.cloned.1.call-start = ((), (), s32[]{:S(2)}) async-start(), calls=%async_computation.4 | async-start | bytes 2621440 | tf_op jit(solution)/shard_map/psum | solution.py:46
  224.7 90.8 %copy-start.1 = (bf16[512,1024]{1,0:T(8,128)(2,1)S(1)}, bf16[512,1024]{1,0:T(8,128)(2,1)}, u32[]{:S(2)}) copy-start(bf16[512,1024]{1,0:T(8,128)(2,1)} %param.6) | copy-start | bytes 3145732
Sparse Core Ops, SparseCore 0:
  37.9 72.6 reduce-scatter.1
  114.0 35.4 all-gather.1
  180.0 44.6 all-reduce.3
  228.8 82.7 all-reduce.5
where the time goes:
time: 326 us; the launch traced here: 322 us
  waiting for transfers between devices  160 us (49%)
  matrix products  86.1 us (26%)
  blocking collectives  45.9 us (14%)
  between operations  13.8 us (4%)
  local copies, waits for them, and re-layouts  12.8 us (4%)
  other arithmetic  3.31 us (1%)
    psum x1, waiting for transfers between devices, shards(): lax.psum((in_replica, out_replica, slope_replica), 'dp')  74.2 us
    reduce_scatter x1, waiting for transfers between devices, shards(): lax.psum_scatter(jnp.dot(act_rows, merged_low, preferred_element_type=jnp...  61.3 us
    psum x1, blocking collectives, shards(): lax.psum((in_replica, out_replica, slope_replica), 'dp')  26.5 us
    psum x1, waiting for transfers between devices, shards(): out_replica = lax.psum(cross_term, 'tensor')  24.1 us
    dot_general x1, matrix products, shards(): in_replica = jnp.dot(full_dir, adapter_out.T, precision=highest)  20.4 us
    dot_general x1, matrix products, shards(): lowrank = jnp.dot(adapter_in, adapter_out, precision=highest)  17.7 us
    dot_general x1, matrix products, shards(): cross_term = jnp.dot(adapter_in.T, full_dir, precision=highest)  15.5 us
    unnamed x18, local copies, waits for them, and re-layouts  12.8 us
  transfers between devices with their start and end apart: 4, of which 3 were waited for; matrix products, arithmetic and copies ran while one was open for 11% of the time, Pallas kernels for 0%

commit v1 on v0

v1 whole, which is shorter than its diff:
```python
import jax
import jax.numpy as jnp
from jax import lax
from jax.sharding import PartitionSpec as P

epsilon = 1e-06
low = jnp.bfloat16
full = jnp.float32


def mm(a, b, ca, cb):
    return lax.dot_general(a, b, (((ca,), (cb,)), ((), ())), preferred_element_type=full)


def two_parts(x):
    high = lax.reduce_precision(x, 8, 7)
    return high.astype(low), (x - high).astype(low)


def bits_of(size):
    bits = [1 << k for k in range(size.bit_length() - 1)]
    assert 1 << len(bits) == size
    return bits


def swap(x, axis, size, bit):
    return lax.ppermute(x, axis, [(i, i ^ bit) for i in range(size)])


def total(x, axis, size):
    for bit in bits_of(size):
        x = x + swap(x, axis, size, bit)
    return x


def scatter_columns(x, axis, size):
    me = lax.axis_index(axis)
    for bit in bits_of(size):
        half = x.shape[1] // 2
        upper = (me & bit) != 0
        left, right = x[:, :half], x[:, half:]
        x = jnp.where(upper, right, left) + swap(jnp.where(upper, left, right), axis, size, bit)
    return x


def gather_columns(x, axis, size):
    me = lax.axis_index(axis)
    for bit in reversed(bits_of(size)):
        upper = (me & bit) != 0
        other = swap(x, axis, size, bit)
        x = jnp.concatenate([jnp.where(upper, other, x), jnp.where(upper, x, other)], axis=1)
    return x


def shards(dp, tp, activations, base_weight, adapter_in, adapter_out, magnitude, cotangent):
    me = lax.axis_index("tensor")
    bits = bits_of(tp)
    order = [0]
    for bit in reversed(bits):
        order = order + [k ^ bit for k in order]
    place = [order.index(k) for k in range(tp)]
    rows = cotangent.shape[0]

    cot = cotangent
    for bit in reversed(bits):
        cot = jnp.concatenate([cot, swap(cot, "tensor", tp, bit)], axis=0)

    b_high, b_low = two_parts(adapter_in)
    a_high, a_low = two_parts(adapter_out)
    lowrank = mm(
        jnp.concatenate([b_high, b_high, b_low], axis=1),
        jnp.concatenate([a_high, a_low, a_high], axis=0),
        1,
        0,
    )
    merged = base_weight.astype(full) + lowrank
    merged_low = merged.astype(low)
    square_sum = total(jnp.sum(merged * merged, axis=0)[None, :], "tensor", tp)
    col_norm = jnp.sqrt(square_sum + epsilon)
    col_scale = magnitude[None, :] / col_norm

    act = jnp.concatenate(
        [lax.dynamic_slice_in_dim(activations, (me ^ k) * rows, rows, 0) for k in order], axis=0
    )
    half = act.shape[0] // 2
    sent = mm(act[half:], merged_low, 1, 0).astype(low)
    kept = mm(act[:half], merged_low, 1, 0)
    slope = (
        jnp.sum(cot[:half].astype(full) * kept, axis=0)
        + jnp.sum(cot[half:].astype(full) * sent.astype(full), axis=0)
    )[None, :]
    summed = kept + swap(sent, "tensor", tp, bits[0]).astype(full)
    for bit in bits[1:]:
        half = summed.shape[0] // 2
        summed = summed[:half] + swap(summed[half:].astype(low), "tensor", tp, bit).astype(full)
    output = (summed * col_scale).astype(low)

    grad_scaled = (cot.astype(full) * col_scale).astype(low)
    act_rel = mm(grad_scaled, merged_low, 1, 1).astype(low)
    places = jnp.asarray(place, jnp.int32)
    grad_act = jnp.concatenate(
        [lax.dynamic_slice_in_dim(act_rel, places[me ^ k] * rows, rows, 0) for k in range(tp)], axis=0
    )

    rank = adapter_in.shape[1]
    fold = lambda x: x[:rank] + x[rank:]
    b_both = jnp.concatenate([b_high, b_low], axis=1)
    a_both = jnp.concatenate([a_high, a_low], axis=0)
    down = fold(mm(b_both, act, 0, 1))
    up = fold(mm(a_both, grad_scaled, 1, 1))
    own_dir = fold(mm(b_both, merged_low, 0, 0))
    out_part = fold(mm(jnp.concatenate(two_parts(down), axis=0), grad_scaled, 1, 0))
    in_part = fold(mm(jnp.concatenate(two_parts(up), axis=0), act, 1, 0))

    slope_replica = total(slope, "tensor", tp)
    norm_coeff = -slope_replica * magnitude[None, :] / (col_norm * col_norm * col_norm)
    out_part = out_part + norm_coeff * own_dir
    in_part = in_part + fold(
        mm(jnp.concatenate(two_parts(adapter_out * norm_coeff), axis=0), merged_low, 1, 1)
    )

    columns = scatter_columns(jnp.concatenate([out_part, slope], axis=0), "tensor", tp)
    stack = jnp.concatenate([in_part, columns], axis=0)
    stack = gather_columns(scatter_columns(stack, "dp", dp), "dp", dp)
    grad_in = stack[:rank].T
    columns = gather_columns(stack[rank:], "tensor", tp)
    grad_out = columns[:rank]
    grad_mag = (columns[rank:] / col_norm)[0]
    return (output, grad_act, grad_in, grad_out, grad_mag)


def solution(mesh):
    dp, tp = mesh.shape["dp"], mesh.shape["tensor"]
    in_specs = (
        P("dp", "tensor"),
        P("tensor", None),
        P("tensor", None),
        P(),
        P(),
        P(("dp", "tensor"), None),
    )
    out_specs = (P(("dp", "tensor"), None), P("dp", "tensor"), P("tensor", None), P(), P())

    def run(*args):
        return shards(dp, tp, *args)

    return jax.shard_map(run, mesh=mesh, in_specs=in_specs, out_specs=out_specs, check_vma=False)
```

time: 326 us -> 139 us (0.43)
  waiting for transfers between devices: 160 us -> 63.5 us
  matrix products: 86.1 us -> 38 us
  blocking collectives: 45.9 us -> 0 us
  starting transfers between devices: 0.38 us -> 19 us
  between operations: 13.8 us -> 3.87 us
  local copies, waits for them, and re-layouts: 12.8 us -> 6.95 us
    psum x2 -> x0, waiting for transfers between devices: 98.3 us -> none  [the longest x1 74.2 us: shards(): lax.psum((in_replica, out_replica, slope_replica), 'dp')]
    ppermute x0 -> x18, waiting for transfers between devices: none -> 63.5 us  [swap(): return lax.ppermute(x, axis, [(i, i ^ bit) for i in range(size)])]
    reduce_scatter x1 -> x0, waiting for transfers between devices: 61.3 us -> none  [shards(): lax.psum_scatter(jnp.dot(act_rows, merged_low, preferred_element_type=jnp...]
    dot_general x6 -> x10, matrix products: 86.1 us -> 38 us  [mm(): lax.dot_general(a, b, (((ca,), (cb,)), ((), ())), preferred_element_type=...]
    psum x3 -> x0, blocking collectives: 45.9 us -> none  [the longest x1 26.5 us: shards(): lax.psum((in_replica, out_replica, slope_replica), 'dp')]
    ppermute x0 -> x18, starting transfers between devices: none -> 19 us  [swap(): return lax.ppermute(x, axis, [(i, i ^ bit) for i in range(size)])]
    unnamed x18 -> x53, local copies, waits for them, and re-layouts: 12.8 us -> 3.43 us
    reduce_sum x1 -> x0, other arithmetic: 3.27 us -> none  [shards(): mag_slope = jnp.sum(cot_float * summed, axis=0) / col_norm]
  transfers between devices with their start and end apart: 4 -> 18, of which waited for: 3 -> 10; matrix products, arithmetic and copies ran while one was open for 11% -> 28% of each run, Pallas kernels for 0% -> 0%
where the time goes in v1:
time: 139 us; the launch traced here: 138 us
  waiting for transfers between devices  63.5 us (46%)
  matrix products  38 us (27%)
  starting transfers between devices  19 us (14%)
  local copies, waits for them, and re-layouts  6.95 us (5%)
  other arithmetic  6.4 us (5%)
  between operations  3.87 us (3%)
    ppermute x18, waiting for transfers between devices, swap(): return lax.ppermute(x, axis, [(i, i ^ bit) for i in range(size)])  63.5 us
    dot_general x10, matrix products, mm(): lax.dot_general(a, b, (((ca,), (cb,)), ((), ())), preferred_element_type=...  38 us
    ppermute x18, starting transfers between devices, swap(): return lax.ppermute(x, axis, [(i, i ^ bit) for i in range(size)])  19 us
    unnamed x53, local copies, waits for them, and re-layouts  3.43 us
  transfers between devices with their start and end apart: 18, of which 10 were waited for; matrix products, arithmetic and copies ran while one was open for 28% of the time, Pallas kernels for 0%

profile of v1, /device:TPU:25, one launch (start us, length us, event | category | flops | bytes accessed | tf_op | source)
XLA Modules:
  0.0 137.7 jit_solution(8906388185260849879)
XLA Ops:
  0.7 1.3 collective-permute-start.4
  2.0 2.3 %constant_dynamic-update-slice_fusion.1 = bf16[256,4096]{1,0:T(8,128)(2,1)} fusion(bf16[128,4096]{1,0:T(8,128)(2,1)} %param.12), kind=kLoop, calls=%fused_computation.118 | loop fusion | bytes 2097152
  4.3 20.7 %collective-permute-done.4 = bf16[128,4096]{1,0:T(8,128)(2,1)S(1)} collective-permute-done((bf16[128,4096]{1,0:T(8,128)(2,1)}, bf16[128,4096]{1,0:T(8,128)(2,1)S(1)}, u32[]{:S(2)}, u32[]{:S(2)}) %collective-permute-start.4) | collective-permute-done | bytes 1048608 | tf_op jit(solution)/shard_map/ppermute | solution.py:27
  27.0 1.5 %collective-permute-start.5 = (bf16[256,4096]{1,0:T(8,128)(2,1)}, bf16[256,4096]{1,0:T(8,128)(2,1)}, u32[]{:S(2)}, u32[]{:S(2)}) collective-permute-start(bf16[256,4096]{1,0:T(8,128)(2,1)} %constant_dynamic-update-slice_fusion), channel_id=1, source_target_pairs={{0,1},{1,0},{2,3},{3,2},{4,5},{5,4},{6,7},{7,6},{8,9},{9,8},{10,11... | collective-permute-start | bytes 6291464 | tf_op jit(solution)/shard_map/ppermute | solution.py:27
  28.9 5.8 %multiply_reduce_fusion = (f32[4096]{0:T(1024)S(1)}, bf16[1024,4096]{1,0:T(8,128)(2,1)S(1)}) fusion(bf16[1024,4096]{1,0:T(8,128)(2,1)} %param.8, bf16[64,4096]{1,0:T(8,128)(2,1)S(1)} %get-tuple-element.22, bf16[64,4096]{1,0:T(8,128)(2,1)S(1)} %get-tuple-element.21, bf16[1024,64]{0,1:T(8,128)(2,1)S(1)} %get-tuple-element.34, ...), kind=kOutput, calls=%fused_computation | convolution fusion | flops 1637478400 | bytes 18104320 | tf_op jit(solution)/shard_map/dot_general | solution.py:12
  34.8 5.6 %multiply_reduce_fusion.1 = (f32[4096]{0:T(1024)S(1)}, bf16[256,4096]{1,0:T(8,128)(2,1)S(1)}) fusion(bf16[256,4096]{1,0:T(8,128)(2,1)} %collective-permute-done.5, bf16[1024,4096]{1,0:T(8,128)(2,1)S(1)} %get-tuple-element.6, bf16[128,1024]{1,0:T(8,128)(2,1)S(1)} %get-tuple-element.20, bf16[128,1024]{1,0:T(8,128)(2,1)S(1)} %get-tuple-element.17), kind=kOutput, calls=%fused_computation.5 | convolution fusion | flops 2153771008 | bytes 13123584 | tf_op jit(solution)/shard_map/dot_general | solution.py:12
  42.2 2.4 %collective-permute-done = bf16[256,4096]{1,0:T(8,128)(2,1)S(1)} collective-permute-done((bf16[256,4096]{1,0:T(8,128)(2,1)S(1)}, bf16[256,4096]{1,0:T(8,128)(2,1)S(1)}, u32[]{:S(2)}, u32[]{:S(2)}) %collective-permute-start) | collective-permute-done | bytes 2097184 | tf_op jit(solution)/shard_map/ppermute | solution.py:27
  44.6 6.4 %multiply_reduce_fusion.2 = (f32[4096]{0:T(1024)S(1)}, f32[256,4096]{1,0:T(8,128)}) fusion(bf16[256,4096]{1,0:T(8,128)(2,1)} %constant_dynamic-update-slice_fusion, bf16[256,4096]{1,0:T(8,128)(2,1)S(1)} %collective-permute-done, bf16[1024,4096]{1,0:T(8,128)(2,1)S(1)} %get-tuple-element.6, bf16[128,1024]{1,0:T(8,128)(2,1)S(1)} %get-tuple-element.18, ...), kind=kOutput, calls=%fused_computation.6 | convolution fusion | flops 2153771008 | bytes 17317888 | tf_op jit(solution)/shard_map/dot_general | solution.py:12
  51.6 1.3 collective-permute-start.3
  54.3 1.3 collective-permute-done.7
  55.7 2.9 %fusion.46 = f32[128,4096]{1,0:T(8,128)S(1)} fusion(bf16[64,512]{1,0:T(8,128)(2,1)S(1)} %get-tuple-element.32, bf16[64,512]{1,0:T(8,128)(2,1)S(1)} %get-tuple-element.31, bf16[256,4096]{1,0:T(8,128)(2,1)} %collective-permute-done.5, bf16[128,4096]{1,0:T(8,128)(2,1)} %copy-done.6, bf16[128,4096]{1,0:T(8,128)(2,1)} %param.12, f32[4096]{0:T(1024)S(1)} %bitcast.23), kind=kOutput, calls=%fused_computation.101 | convolution fusion | flops 553910272 | bytes 6438912 | tf_op jit(solution)/shard_map/dot_general | solution.py:12
  59.3 1.9 %collective-permute-start.8 = (f32[65,2048]{1,0:T(8,128)S(1)}, f32[65,2048]{1,0:T(8,128)S(1)}, u32[]{:S(2)}, u32[]{:S(2)}) collective-permute-start(f32[65,2048]{1,0:T(8,128)S(1)} %broadcast_select_fusion.2), channel_id=1, source_target_pairs={{0,1},{1,0},{2,3},{3,2},{4,5},{5,4},{6,7},{7,6},{8,9},{9,8},{10,11... | collective-permute-start | bytes 1597448 | tf_op jit(solution)/shard_map/ppermute | solution.py:27
  61.1 3.9 %fusion.14 = f32[128,512]{1,0:T(8,128)S(1)} fusion(bf16[64,4096]{1,0:T(8,128)(2,1)S(1)} %copy-done.10, bf16[64,4096]{1,0:T(8,128)(2,1)S(1)} %copy-done.12, bf16[256,4096]{1,0:T(8,128)(2,1)} %collective-permute-done.5, bf16[128,4096]{1,0:T(8,128)(2,1)S(1)} %copy-done.7, bf16[128,4096]{1,0:T(8,128)(2,1)S(1)} %copy-done.4, f32[4096]{0:T(1024)S(1)} %bitcast.24), kind=kOutput, calls=%fused_computation.35 | convolution fusion | flops 555745280 | bytes 5521408 | tf_op jit(solution)/shard_map/dot_general | solution.py:12
  65.2 2.9 %fusion.18 = f32[128,1024]{1,0:T(8,128)S(1)} fusion(bf16[1024,4096]{1,0:T(8,128)(2,1)S(1)} %bitcast.18, bf16[64,4096]{1,0:T(8,128)(2,1)S(1)} %get-tuple-element.12, bf16[64,4096]{1,0:T(8,128)(2,1)S(1)} %get-tuple-element.11), kind=kOutput, calls=%fused_computation.40 | convolution fusion | flops 1075838976 | bytes 9961472 | tf_op jit(solution)/shard_map/dot_general | solution.py:12
  68.9 6.7 %collective-permute-done.9 = f32[65,1024]{1,0:T(8,128)S(1)} collective-permute-done((f32[65,1024]{1,0:T(8,128)S(1)}, f32[65,1024]{1,0:T(8,128)S(1)}, u32[]{:S(2)}, u32[]{:S(2)}) %collective-permute-start.9) | collective-permute-done | bytes 266272 | tf_op jit(solution)/shard_map/ppermute | solution.py:27
  77.0 4.8 %collective-permute-done.10 = f32[129,512]{1,0:T(8,128)S(1)} collective-permute-done((f32[129,512]{1,0:T(8,128)S(1)}, f32[129,512]{1,0:T(8,128)S(1)}, u32[]{:S(2)}, u32[]{:S(2)}) %collective-permute-start.10) | collective-permute-done | bytes 264224 | tf_op jit(solution)/shard_map/ppermute | solution.py:27
  82.2 3.7 %collective-permute-done.11 = f32[129,256]{1,0:T(8,128)S(1)} collective-permute-done((f32[129,256]{1,0:T(8,128)S(1)}, f32[129,256]{1,0:T(8,128)S(1)}, u32[]{:S(2)}, u32[]{:S(2)}) %collective-permute-start.11) | collective-permute-done | bytes 132128 | tf_op jit(solution)/shard_map/ppermute | solution.py:27
  86.1 4.6 %collective-permute-done.12 = f32[129,128]{1,0:T(8,128)S(1)} collective-permute-done((f32[129,128]{1,0:T(8,128)S(1)}, f32[129,128]{1,0:T(8,128)S(1)}, u32[]{:S(2)}, u32[]{:S(2)}) %collective-permute-start.12) | collective-permute-done | bytes 66080 | tf_op jit(solution)/shard_map/ppermute | solution.py:27
  90.9 5.8 %collective-permute-done.13 = f32[129,128]{1,0:T(8,128)S(1)} collective-permute-done((f32[129,128]{1,0:T(8,128)S(1)}, f32[129,128]{1,0:T(8,128)S(1)}, u32[]{:S(2)}, u32[]{:S(2)}) %collective-permute-start.13) | collective-permute-done | bytes 66080 | tf_op jit(solution)/shard_map/ppermute | solution.py:27
  100.1 1.7 %slice.233 = bf16[128,4096]{1,0:T(8,128)(2,1)S(1)} slice(f32[256,4096]{1,0:T(8,128)} %get-tuple-element.8), slice={[128:256], [0:4096]} | slice | bytes 2097152 | tf_op jit(solution)/shard_map/slice | solution.py:95
  103.4 8.5 %convolution_convert_fusion.1 = bf16[512,1024]{1,0:T(8,128)(2,1)S(1)} fusion(bf16[1024,4096]{1,0:T(8,128)(2,1)} %copy-done, bf16[256,4096]{1,0:T(8,128)(2,1)} %collective-permute-done.5, bf16[128,4096]{1,0:T(8,128)(2,1)S(1)} %copy-done.8, bf16[128,4096]{1,0:T(8,128)(2,1)S(1)} %copy-done.5, f32[4096]{0:T(1024)S(1)} %bitcast.25), kind=kOutput, calls=%fused_computation.22 | convolution fusion | flops 4312268800 | bytes 13647872 | tf_op jit(solution)/shard_map/dot_general | solution.py:12
  112.1 1.3 collective-permute-start.16
  114.5 12.6 %collective-permute-done.16 = f32[65,1024]{1,0:T(8,128)S(1)} collective-permute-done((f32[65,1024]{1,0:T(8,128)S(1)}, f32[65,1024]{1,0:T(8,128)S(1)}, u32[]{:S(2)}, u32[]{:S(2)}) %collective-permute-start.16) | collective-permute-done | bytes 266272 | tf_op jit(solution)/shard_map/ppermute | solution.py:27
  127.3 6.7 %collective-permute-start.17 = (f32[65,2048]{1,0:T(8,128)S(1)}, f32[65,2048]{1,0:T(8,128)S(1)}, u32[]{:S(2)}, u32[]{:S(2)}) collective-permute-start(f32[65,2048]{1,0:T(8,128)S(1)} %pad_maximum_fusion.3), channel_id=1, source_target_pairs={{0,1},{1,0},{2,3},{3,2},{4,5},{5,4},{6,7},{7,6},{8,9},{9,8},{10,11... | collective-permute-start | bytes 1597448 | tf_op jit(solution)/shard_map/ppermute | solution.py:27
  (115 shorter events, 17.1 us)
Async XLA Ops:
  0.6 27.9 %copy-start.21 = (f32[1024,64]{0,1:T(8,128)S(1)}, f32[1024,64]{0,1:T(8,128)}, u32[]{:S(2)}) copy-start(f32[1024,64]{0,1:T(8,128)} %param.9) | copy-start | bytes 786436
  0.6 28.0 %copy-start.3 = (bf16[512,1024]{1,0:T(8,128)(2,1)S(1)}, bf16[512,1024]{1,0:T(8,128)(2,1)}, u32[]{:S(2)}) copy-start(bf16[512,1024]{1,0:T(8,128)(2,1)} %param.7) | copy-start | bytes 3145732
  0.7 28.1 %copy-start.1 = (f32[64,4096]{1,0:T(8,128)S(1)}, f32[64,4096]{1,0:T(8,128)}, u32[]{:S(2)}) copy-start(f32[64,4096]{1,0:T(8,128)} %param.10) | copy-start | bytes 3145732
  0.7 24.3 %collective-permute-start.4 = (bf16[128,4096]{1,0:T(8,128)(2,1)}, bf16[128,4096]{1,0:T(8,128)(2,1)S(1)}, u32[]{:S(2)}, u32[]{:S(2)}) collective-permute-start(bf16[128,4096]{1,0:T(8,128)(2,1)} %param.12), channel_id=1, source_target_pairs={{0,2},{1,3},{2,0},{3,1},{4,6},{5,7},{6,4},{7,5},{8,10},{9,11},{10,... | collective-permute-start | bytes 3145736 | tf_op jit(solution)/shard_map/ppermute | solution.py:27
  27.0 7.8 %collective-permute-start.5 = (bf16[256,4096]{1,0:T(8,128)(2,1)}, bf16[256,4096]{1,0:T(8,128)(2,1)}, u32[]{:S(2)}, u32[]{:S(2)}) collective-permute-start(bf16[256,4096]{1,0:T(8,128)(2,1)} %constant_dynamic-update-slice_fusion), channel_id=1, source_target_pairs={{0,1},{1,0},{2,3},{3,2},{4,5},{5,4},{6,7},{7,6},{8,9},{9,8},{10,11... | collective-permute-start | bytes 6291464 | tf_op jit(solution)/shard_map/ppermute | solution.py:27
  40.4 4.2 %collective-permute-start = (bf16[256,4096]{1,0:T(8,128)(2,1)S(1)}, bf16[256,4096]{1,0:T(8,128)(2,1)S(1)}, u32[]{:S(2)}, u32[]{:S(2)}) collective-permute-start(bf16[256,4096]{1,0:T(8,128)(2,1)S(1)} %get-tuple-element.45), channel_id=1, source_target_pairs={{0,1},{1,0},{2,3},{3,2},{4,5},{5,4},{6,7},{7,6},{8,9},{9,8},{10,11... | collective-permute-start | bytes 6291464 | tf_op jit(solution)/shard_map/ppermute | solution.py:27
  40.4 11.2 %collective-permute-start.2 = (f32[1,4096]{1,0:T(1,128)S(1)}, f32[1,4096]{1,0:T(1,128)S(1)}, u32[]{:S(2)}, u32[]{:S(2)}) collective-permute-start(f32[1,4096]{1,0:T(1,128)S(1)} %bitcast.30), channel_id=1, source_target_pairs={{0,1},{1,0},{2,3},{3,2},{4,5},{5,4},{6,7},{7,6},{8,9},{9,8},{10,11... | collective-permute-start | bytes 49160 | tf_op jit(solution)/shard_map/ppermute | solution.py:27
  51.0 2.0 %collective-permute-start.6 = (f32[1,4096]{1,0:T(1,128)S(1)}, f32[1,4096]{1,0:T(1,128)S(1)}, u32[]{:S(2)}, u32[]{:S(2)}) collective-permute-start(f32[1,4096]{1,0:T(1,128)S(1)} %bitcast.19), channel_id=1, source_target_pairs={{0,1},{1,0},{2,3},{3,2},{4,5},{5,4},{6,7},{7,6},{8,9},{9,8},{10,11... | collective-permute-start | bytes 49160 | tf_op jit(solution)/shard_map/ppermute | solution.py:27
  51.6 2.7 %collective-permute-start.3 = (f32[1,4096]{1,0:T(1,128)S(1)}, f32[1,4096]{1,0:T(1,128)S(1)}, u32[]{:S(2)}, u32[]{:S(2)}) collective-permute-start(f32[1,4096]{1,0:T(1,128)S(1)} %add.122), channel_id=1, source_target_pairs={{0,2},{1,3},{2,0},{3,1},{4,6},{5,7},{6,4},{7,5},{8,10},{9,11},{10,... | collective-permute-start | bytes 49160 | tf_op jit(solution)/shard_map/ppermute | solution.py:27
  53.0 2.7 %collective-permute-start.7 = (f32[1,4096]{1,0:T(1,128)S(1)}, f32[1,4096]{1,0:T(1,128)S(1)}, u32[]{:S(2)}, u32[]{:S(2)}) collective-permute-start(f32[1,4096]{1,0:T(1,128)S(1)} %add.138), channel_id=1, source_target_pairs={{0,2},{1,3},{2,0},{3,1},{4,6},{5,7},{6,4},{7,5},{8,10},{9,11},{10,... | collective-permute-start | bytes 49160 | tf_op jit(solution)/shard_map/ppermute | solution.py:27
  59.3 8.8 %collective-permute-start.8 = (f32[65,2048]{1,0:T(8,128)S(1)}, f32[65,2048]{1,0:T(8,128)S(1)}, u32[]{:S(2)}, u32[]{:S(2)}) collective-permute-start(f32[65,2048]{1,0:T(8,128)S(1)} %broadcast_select_fusion.2), channel_id=1, source_target_pairs={{0,1},{1,0},{2,3},{3,2},{4,5},{5,4},{6,7},{7,6},{8,9},{9,8},{10,11... | collective-permute-start | bytes 1597448 | tf_op jit(solution)/shard_map/ppermute | solution.py:27
  68.2 7.4 %collective-permute-start.9 = (f32[65,1024]{1,0:T(8,128)S(1)}, f32[65,1024]{1,0:T(8,128)S(1)}, u32[]{:S(2)}, u32[]{:S(2)}) collective-permute-start(f32[65,1024]{1,0:T(8,128)S(1)} %slice_select_fusion), channel_id=1, source_target_pairs={{0,2},{1,3},{2,0},{3,1},{4,6},{5,7},{6,4},{7,5},{8,10},{9,11},{10,... | collective-permute-start | bytes 798728 | tf_op jit(solution)/shard_map/ppermute | solution.py:27
  68.8 28.0 %copy-start.23 = (s32[4]{0:T(128)S(1)}, s32[4]{0:T(128)}, u32[]{:S(2)}) copy-start(s32[4]{0:T(128)} %constant.34.clone) | copy-start | bytes 52
  75.7 6.1 %collective-permute-start.10 = (f32[129,512]{1,0:T(8,128)S(1)}, f32[129,512]{1,0:T(8,128)S(1)}, u32[]{:S(2)}, u32[]{:S(2)}) collective-permute-start(f32[129,512]{1,0:T(8,128)S(1)} %broadcast_select_fusion.7), channel_id=1, source_target_pairs={{0,4},{4,0},{8,12},{12,8},{16,20},{20,16},{24,28},{28,24},{1,5},{5... | collective-permute-start | bytes 792584 | tf_op jit(solution)/shard_map/ppermute | solution.py:27
  77.0 26.4 %copy-start.5 = (bf16[128,4096]{1,0:T(8,128)(2,1)S(1)}, bf16[128,4096]{1,0:T(8,128)(2,1)}, u32[]{:S(2)}) copy-start(bf16[128,4096]{1,0:T(8,128)(2,1)} %param.12) | copy-start | bytes 3145732
  77.0 26.4 %copy-start.8 = (bf16[128,4096]{1,0:T(8,128)(2,1)S(1)}, bf16[128,4096]{1,0:T(8,128)(2,1)}, u32[]{:S(2)}) copy-start(bf16[128,4096]{1,0:T(8,128)(2,1)} %copy-done.6) | copy-start | bytes 3145732
  81.9 4.0 %collective-permute-start.11 = (f32[129,256]{1,0:T(8,128)S(1)}, f32[129,256]{1,0:T(8,128)S(1)}, u32[]{:S(2)}, u32[]{:S(2)}) collective-permute-start(f32[129,256]{1,0:T(8,128)S(1)} %slice_select_fusion.1), channel_id=1, source_target_pairs={{0,8},{4,12},{8,0},{12,4},{16,24},{20,28},{24,16},{28,20},{1,9},{5... | collective-permute-start | bytes 396296 | tf_op jit(solution)/shard_map/ppermute | solution.py:27
  86.0 4.8 %collective-permute-start.12 = (f32[129,128]{1,0:T(8,128)S(1)}, f32[129,128]{1,0:T(8,128)S(1)}, u32[]{:S(2)}, u32[]{:S(2)}) collective-permute-start(f32[129,128]{1,0:T(8,128)S(1)} %slice_select_fusion.2), channel_id=1, source_target_pairs={{0,16},{4,20},{8,24},{12,28},{16,0},{20,4},{24,8},{28,12},{1,17},{... | collective-permute-start | bytes 198152 | tf_op jit(solution)/shard_map/ppermute | solution.py:27
  90.7 6.0 %collective-permute-start.13 = (f32[129,128]{1,0:T(8,128)S(1)}, f32[129,128]{1,0:T(8,128)S(1)}, u32[]{:S(2)}, u32[]{:S(2)}) collective-permute-start(f32[129,128]{1,0:T(8,128)S(1)} %select_add_fusion.4), channel_id=1, source_target_pairs={{0,16},{4,20},{8,24},{12,28},{16,0},{20,4},{24,8},{28,12},{1,17},{... | collective-permute-start | bytes 198152 | tf_op jit(solution)/shard_map/ppermute | solution.py:27
  96.7 5.3 %collective-permute-start.14 = (f32[129,256]{1,0:T(8,128)S(1)}, f32[129,256]{1,0:T(8,128)S(1)}, u32[]{:S(2)}, u32[]{:S(2)}) collective-permute-start(f32[129,256]{1,0:T(8,128)S(1)} %pad_maximum_fusion.12), channel_id=1, source_target_pairs={{0,8},{4,12},{8,0},{12,4},{16,24},{20,28},{24,16},{28,20},{1,9},{5... | collective-permute-start | bytes 396296 | tf_op jit(solution)/shard_map/ppermute | solution.py:27
  101.8 32.1 %collective-permute-start.1 = (bf16[128,4096]{1,0:T(8,128)(2,1)S(1)}, bf16[128,4096]{1,0:T(8,128)(2,1)S(1)}, u32[]{:S(2)}, u32[]{:S(2)}) collective-permute-start(bf16[128,4096]{1,0:T(8,128)(2,1)S(1)} %slice.233), channel_id=1, source_target_pairs={{0,2},{1,3},{2,0},{3,1},{4,6},{5,7},{6,4},{7,5},{8,10},{9,11},{10,... | collective-permute-start | bytes 3145736 | tf_op jit(solution)/shard_map/ppermute | solution.py:27
  102.1 9.9 %collective-permute-start.15 = (f32[129,512]{1,0:T(8,128)S(1)}, f32[129,512]{1,0:T(8,128)S(1)}, u32[]{:S(2)}, u32[]{:S(2)}) collective-permute-start(f32[129,512]{1,0:T(8,128)S(1)} %pad_maximum_fusion.6), channel_id=1, source_target_pairs={{0,4},{4,0},{8,12},{12,8},{16,20},{20,16},{24,28},{28,24},{1,5},{5... | collective-permute-start | bytes 792584 | tf_op jit(solution)/shard_map/ppermute | solution.py:27
  112.1 15.1 %collective-permute-start.16 = (f32[65,1024]{1,0:T(8,128)S(1)}, f32[65,1024]{1,0:T(8,128)S(1)}, u32[]{:S(2)}, u32[]{:S(2)}) collective-permute-start(f32[65,1024]{1,0:T(8,128)S(1)} %pad_maximum_fusion.4), channel_id=1, source_target_pairs={{0,2},{1,3},{2,0},{3,1},{4,6},{5,7},{6,4},{7,5},{8,10},{9,11},{10,... | collective-permute-start | bytes 798728 | tf_op jit(solution)/shard_map/ppermute | solution.py:27
  127.3 8.7 %collective-permute-start.17 = (f32[65,2048]{1,0:T(8,128)S(1)}, f32[65,2048]{1,0:T(8,128)S(1)}, u32[]{:S(2)}, u32[]{:S(2)}) collective-permute-start(f32[65,2048]{1,0:T(8,128)S(1)} %pad_maximum_fusion.3), channel_id=1, source_target_pairs={{0,1},{1,0},{2,3},{3,2},{4,5},{5,4},{6,7},{7,6},{8,9},{9,8},{10,11... | collective-permute-start | bytes 1597448 | tf_op jit(solution)/shard_map/ppermute | solution.py:27
  (20 other events, 173.6 us)

commit v2 on v1

--- a/solution.py
+++ b/solution.py
@@ -1,6 +1,10 @@
+import functools
+
 import jax
 import jax.numpy as jnp
 from jax import lax
+from jax.experimental import pallas as pl
+from jax.experimental.pallas import tpu as pltpu
 from jax.sharding import PartitionSpec as P
 
 epsilon = 1e-06
@@ -10,6 +14,10 @@
 
 def mm(a, b, ca, cb):
     return lax.dot_general(a, b, (((ca,), (cb,)), ((), ())), preferred_element_type=full)
+
+
+def tie(*arrays):
+    return lax.optimization_barrier(arrays)
 
 
 def two_parts(x):
@@ -33,23 +41,84 @@
     return x
 
 
-def scatter_columns(x, axis, size):
+def greet(axis, size):
     me = lax.axis_index(axis)
-    for bit in bits_of(size):
-        half = x.shape[1] // 2
-        upper = (me & bit) != 0
-        left, right = x[:, :half], x[:, half:]
-        x = jnp.where(upper, right, left) + swap(jnp.where(upper, left, right), axis, size, bit)
-    return x
-
-
-def gather_columns(x, axis, size):
-    me = lax.axis_index(axis)
-    for bit in reversed(bits_of(size)):
-        upper = (me & bit) != 0
-        other = swap(x, axis, size, bit)
-        x = jnp.concatenate([jnp.where(upper, other, x), jnp.where(upper, x, other)], axis=1)
-    return x
+    barrier = pltpu.get_barrier_semaphore()
+    for k in range(1, size):
+        pl.semaphore_signal(
+            barrier,
+            inc=1,
+            device_id={axis: lax.rem(me + k, size)},
+            device_id_type=pl.DeviceIdType.MESH,
+        )
+    pl.semaphore_wait(barrier, size - 1)
+    return me
+
+
+def send_all(axis, size, me, source, slots, sends, recvs):
+    copies = []
+    for k in range(1, size):
+        peer = lax.rem(me + k, size)
+        copy = pltpu.make_async_remote_copy(
+            src_ref=source(peer),
+            dst_ref=slots.at[me],
+            send_sem=sends.at[k - 1],
+            recv_sem=recvs.at[k - 1],
+            device_id={axis: peer},
+            device_id_type=pl.DeviceIdType.MESH,
+        )
+        copy.start()
+        copies.append(copy)
+    return copies
+
+
+def exchange_kernel(axis, size, scatter, gather, x_ref, o_ref, *scratch):
+    me = greet(axis, size)
+    mine = x_ref
+    if scatter:
+        slots, sends, recvs, *scratch = scratch
+        copies = send_all(axis, size, me, lambda p: x_ref.at[p], slots, sends, recvs)
+        slots[me] = x_ref[me]
+        for copy in copies:
+            copy.wait()
+        sums = slots[0].astype(full)
+        for k in range(1, size):
+            sums = sums + slots[k].astype(full)
+        if not gather:
+            o_ref[...] = sums
+            return
+        mine, *scratch = scratch
+        mine[...] = sums.astype(low)
+    slots, sends, recvs = scratch
+    copies = send_all(axis, size, me, lambda p: mine, slots, sends, recvs)
+    slots[me] = mine[...]
+    for copy in copies:
+        copy.wait()
+    o_ref[...] = slots[...].astype(full)
+
+
+def exchange(x, axis, size, scatter, gather, ident):
+    block = x.shape[1:] if scatter else x.shape
+    group = [
+        pltpu.VMEM((size, *block), low),
+        pltpu.SemaphoreType.DMA((size - 1,)),
+        pltpu.SemaphoreType.DMA((size - 1,)),
+    ]
+    scratch = group if scatter else []
+    if scatter and gather:
+        scratch = scratch + [pltpu.VMEM(block, low)]
+    if gather:
+        scratch = scratch + group
+    return pl.pallas_call(
+        functools.partial(exchange_kernel, axis, size, scatter, gather),
+        out_shape=jax.ShapeDtypeStruct((size, *block) if gather else block, full),
+        in_specs=[pl.BlockSpec(memory_space=pltpu.VMEM)],
+        out_specs=pl.BlockSpec(memory_space=pltpu.VMEM),
+        scratch_shapes=scratch,
+        compiler_params=pltpu.CompilerParams(
+            collective_id=ident, has_side_effects=True, vmem_limit_bytes=24 * 2**20
+        ),
+    )(x)
 
 
 def shards(dp, tp, activations, base_weight, adapter_in, adapter_out, magnitude, cotangent):
@@ -61,9 +130,13 @@
     place = [order.index(k) for k in range(tp)]
     rows = cotangent.shape[0]
 
-    cot = cotangent
-    for bit in reversed(bits):
-        cot = jnp.concatenate([cot, swap(cot, "tensor", tp, bit)], axis=0)
+    quarter = rows // 4
+    quarters = []
+    for i in range(4):
+        part = cotangent[i * quarter : (i + 1) * quarter]
+        for bit in reversed(bits[1:]):
+            part = jnp.concatenate([part, swap(part, "tensor", tp, bit)], axis=0)
+        quarters.append(part)
 
     b_high, b_low = two_parts(adapter_in)
     a_high, a_low = two_parts(adapter_out)
@@ -74,7 +147,7 @@
         0,
     )
     merged = base_weight.astype(full) + lowrank
-    merged_low = merged.astype(low)
+    merged_low, quarters[0] = tie(merged.astype(low), quarters[0])
     square_sum = total(jnp.sum(merged * merged, axis=0)[None, :], "tensor", tp)
     col_norm = jnp.sqrt(square_sum + epsilon)
     col_scale = magnitude[None, :] / col_norm
@@ -84,19 +157,30 @@
     )
     half = act.shape[0] // 2
     sent = mm(act[half:], merged_low, 1, 0).astype(low)
+    merged_low, sent, quarters[1] = tie(merged_low, sent, quarters[1])
     kept = mm(act[:half], merged_low, 1, 0)
+    kept, quarters[2] = tie(kept, quarters[2])
+    summed = kept + swap(sent, "tensor", tp, bits[0]).astype(full)
+    for bit in bits[1:-1]:
+        half = summed.shape[0] // 2
+        summed = summed[:half] + swap(summed[half:].astype(low), "tensor", tp, bit).astype(full)
+    passed, own = summed[rows:].astype(low), summed[:rows]
+    passed, own, quarters[3] = tie(passed, own, quarters[3])
+    arrived = [
+        swap(passed[i * quarter : (i + 1) * quarter], "tensor", tp, bits[-1]) for i in range(4)
+    ]
+    cot = jnp.concatenate([part.reshape(-1, quarter, part.shape[1]) for part in quarters], axis=1)
+    cot = cot.reshape(-1, cot.shape[2])
+    cot = jnp.concatenate([cot, swap(cot, "tensor", tp, bits[0])], axis=0)
+    half = kept.shape[0]
     slope = (
         jnp.sum(cot[:half].astype(full) * kept, axis=0)
         + jnp.sum(cot[half:].astype(full) * sent.astype(full), axis=0)
     )[None, :]
-    summed = kept + swap(sent, "tensor", tp, bits[0]).astype(full)
-    for bit in bits[1:]:
-        half = summed.shape[0] // 2
-        summed = summed[:half] + swap(summed[half:].astype(low), "tensor", tp, bit).astype(full)
-    output = (summed * col_scale).astype(low)
-
-    grad_scaled = (cot.astype(full) * col_scale).astype(low)
+    slope, cot, arrived[0] = tie(slope, cot, arrived[0])
+    grad_scaled, arrived[1] = tie((cot.astype(full) * col_scale).astype(low), arrived[1])
     act_rel = mm(grad_scaled, merged_low, 1, 1).astype(low)
+    act_rel, grad_scaled, arrived[2] = tie(act_rel, grad_scaled, arrived[2])
     places = jnp.asarray(place, jnp.int32)
     grad_act = jnp.concatenate(
         [lax.dynamic_slice_in_dim(act_rel, places[me ^ k] * rows, rows, 0) for k in range(tp)], axis=0
@@ -115,17 +199,34 @@
     slope_replica = total(slope, "tensor", tp)
     norm_coeff = -slope_replica * magnitude[None, :] / (col_norm * col_norm * col_norm)
     out_part = out_part + norm_coeff * own_dir
+    out_part, in_part, norm_coeff, arrived[3] = tie(out_part, in_part, norm_coeff, arrived[3])
     in_part = in_part + fold(
         mm(jnp.concatenate(two_parts(adapter_out * norm_coeff), axis=0), merged_low, 1, 1)
     )
 
-    columns = scatter_columns(jnp.concatenate([out_part, slope], axis=0), "tensor", tp)
-    stack = jnp.concatenate([in_part, columns], axis=0)
-    stack = gather_columns(scatter_columns(stack, "dp", dp), "dp", dp)
+    out_part, in_part, grad_act = tie(out_part, in_part, grad_act)
+    output = ((own + jnp.concatenate(arrived, axis=0).astype(full)) * col_scale).astype(low)
+    wide = out_part.shape[1]
+    block = wide // tp
+    padded = jnp.concatenate([out_part, slope, jnp.zeros((15, wide), full)], axis=0).astype(low)
+    extra = padded.shape[0]
+    columns = exchange(
+        padded.reshape(extra, tp, block).transpose(1, 0, 2), "tensor", tp, True, False, 0
+    )
+    stack = jnp.concatenate([in_part, columns], axis=0).astype(low)
+    high = stack.shape[0]
+    unit = dp * 16 * 128
+    count = -(-stack.size // unit) * unit
+    flat = stack.reshape(high, block // 128, 128).transpose(1, 0, 2).reshape(-1, 128)
+    flat = jnp.pad(flat, ((0, count // 128 - flat.shape[0]), (0, 0)))
+    flat = exchange(flat.reshape(dp, -1, 128), "dp", dp, True, True, 1).reshape(-1, 128)
+    flat = flat[: stack.size // 128].reshape(block // 128, high, 128)
+    stack = flat.transpose(1, 0, 2).reshape(high, block)
     grad_in = stack[:rank].T
-    columns = gather_columns(stack[rank:], "tensor", tp)
+    columns = exchange(stack[rank:].astype(low), "tensor", tp, False, True, 2)
+    columns = columns.transpose(1, 0, 2).reshape(extra, wide)
     grad_out = columns[:rank]
-    grad_mag = (columns[rank:] / col_norm)[0]
+    grad_mag = (columns[rank : rank + 1] / col_norm)[0]
     return (output, grad_act, grad_in, grad_out, grad_mag)
 
 

time: 139 us -> 128 us (0.921); the launches traced: 138 us -> 128 us
  waiting for transfers between devices: 63.5 us -> 15.6 us
  Pallas kernels: 0 us -> 41.4 us
  starting transfers between devices: 19 us -> 12.3 us
  other arithmetic: 6.4 us -> 11.9 us
  matrix products: 38 us -> 33.8 us
  local copies, waits for them, and re-layouts: 6.95 us -> 9.41 us
    ppermute x18 -> x14, waiting for transfers between devices: 63.5 us -> 15.6 us  [swap(): return lax.ppermute(x, axis, [(i, i ^ bit) for i in range(size)])]
    pallas_call x0 -> x3, Pallas kernels: none -> 41.4 us  [exchange(): pl.pallas_call(functools.partial(exchange_kernel, axis, size, scatter, ga...]
    ppermute x18 -> x14, starting transfers between devices: 19 us -> 12.3 us  [swap(): return lax.ppermute(x, axis, [(i, i ^ bit) for i in range(size)])]
    dot_general x10, matrix products: 38 us -> 33.8 us  [mm(): lax.dot_general(a, b, (((ca,), (cb,)), ((), ())), preferred_element_type=...]
    concatenate x5 -> x7, other arithmetic: 1.15 us -> 5.06 us  [the longest x1 2.43 us: shards(): cot = jnp.concatenate([cot, swap(cot, 'tensor', tp, bits[0])], axis=0)]
    slice x1 -> x7, local copies, waits for them, and re-layouts: 1.71 us -> 3.39 us  [the longest x1 1.36 us: shards(): part = cotangent[i * quarter:(i + 1) * quarter]]
    unnamed x53 -> x47, local copies, waits for them, and re-layouts: 3.43 us -> 4.31 us
  transfers between devices with their start and end apart: 18 -> 14, of which waited for: 10 -> 5; matrix products, arithmetic and copies ran while one was open for 28% -> 30% of each run, Pallas kernels for 0% -> 0%
where the time goes in v2:
time: 128 us
  Pallas kernels  41.4 us (32%)
  matrix products  33.8 us (26%)
  waiting for transfers between devices  15.6 us (12%)
  starting transfers between devices  12.3 us (10%)
  other arithmetic  11.9 us (9%)
  local copies, waits for them, and re-layouts  9.41 us (7%)
  between operations  3.79 us (3%)
    pallas_call x3, Pallas kernels, exchange(): pl.pallas_call(functools.partial(exchange_kernel, axis, size, scatter, ga...  41.4 us
    dot_general x10, matrix products, mm(): lax.dot_general(a, b, (((ca,), (cb,)), ((), ())), preferred_element_type=...  33.8 us
    ppermute x14, waiting for transfers between devices, swap(): return lax.ppermute(x, axis, [(i, i ^ bit) for i in range(size)])  15.6 us
    ppermute x14, starting transfers between devices, swap(): return lax.ppermute(x, axis, [(i, i ^ bit) for i in range(size)])  12.3 us
    unnamed x47, local copies, waits for them, and re-layouts  4.31 us
  transfers between devices with their start and end apart: 14, of which 5 were waited for; matrix products, arithmetic and copies ran while one was open for 30% of the time, Pallas kernels for 0%

profile of v2, /device:TPU:25, one launch (start us, length us, event | category | flops | bytes accessed | tf_op | source)
XLA Modules:
  0.0 128.2 jit_solution(11518993830043770541)
XLA Ops:
  0.7 1.4 %fusion.59 = (bf16[32,4096]{1,0:T(8,128)(2,1)S(1)}, bf16[32,4096]{1,0:T(8,128)(2,1)S(1)}, bf16[32,4096]{1,0:T(8,128)(2,1)S(1)}, bf16[32,4096]{1,0:T(8,128)(2,1)S(1)}) fusion(bf16[128,4096]{1,0:T(8,128)(2,1)} %param.12), kind=kLoop, calls=%fused_computation.116 | loop fusion | bytes 2097152 | tf_op jit(solution)/shard_map/slice | solution.py:136
  2.0 1.3 %collective-permute-start = (bf16[32,4096]{1,0:T(8,128)(2,1)S(1)}, bf16[32,4096]{1,0:T(8,128)(2,1)}, u32[]{:S(2)}, u32[]{:S(2)}) collective-permute-start(bf16[32,4096]{1,0:T(8,128)(2,1)S(1)} %get-tuple-element.69), channel_id=1, source_target_pairs={{0,2},{1,3},{2,0},{3,1},{4,6},{5,7},{6,4},{7,5},{8,10},{9,11},{10,... | collective-permute-start | bytes 786440 | tf_op jit(solution)/shard_map/ppermute | solution.py:35
  3.8 7.6 %multiply_reduce_fusion = (f32[4096]{0:T(1024)S(1)}, bf16[1024,4096]{1,0:T(8,128)(2,1)}) fusion(bf16[1024,4096]{1,0:T(8,128)(2,1)} %param.8, bf16[64,4096]{1,0:T(8,128)(2,1)S(1)} %get-tuple-element.76, bf16[64,4096]{1,0:T(8,128)(2,1)S(1)} %get-tuple-element.75, bf16[1024,64]{0,1:T(8,128)(2,1)S(1)} %get-tuple-element.82, bf16[1024,64]{0,1:T(8,128)(2,1)S(1)} %get-tuple-element.81), kind=kOutput, calls=%fused_computation | convolution fusion | flops 1637478400 | bytes 18104320 | tf_op jit(solution)/shard_map/dot_general | solution.py:16
  11.6 1.3 %pad_maximum_fusion.4 = bf16[64,4096]{1,0:T(8,128)(2,1)S(1)} fusion(bf16[32,4096]{1,0:T(8,128)(2,1)} %collective-permute-done, bf16[32,4096]{1,0:T(8,128)(2,1)S(1)} %get-tuple-element.69), kind=kLoop, calls=%fused_computation.46 | loop fusion | flops 1048576 | bytes 1048576 | tf_op jit(solution)/shard_map/concatenate | solution.py:138
  12.9 6.0 %convolution_convert_fusion = bf16[256,4096]{1,0:T(8,128)(2,1)S(1)} fusion(bf16[1024,4096]{1,0:T(8,128)(2,1)} %get-tuple-element.31, bf16[128,1024]{1,0:T(8,128)(2,1)S(1)} %get-tuple-element.73, bf16[128,1024]{1,0:T(8,128)(2,1)S(1)} %get-tuple-element.74), kind=kOutput, calls=%fused_computation.4 | convolution fusion | flops 2149580800 | bytes 11010048 | tf_op jit(solution)/shard_map/dot_general | solution.py:16
  20.0 1.3 %collective-permute-start.3 = (bf16[256,4096]{1,0:T(8,128)(2,1)S(1)}, bf16[256,4096]{1,0:T(8,128)(2,1)S(1)}, u32[]{:S(2)}, u32[]{:S(2)}) collective-permute-start(bf16[256,4096]{1,0:T(8,128)(2,1)S(1)} %convolution_convert_fusion), channel_id=1, source_target_pairs={{0,1},{1,0},{2,3},{3,2},{4,5},{5,4},{6,7},{7,6},{8,9},{9,8},{10,11... | collective-permute-start | bytes 6291464 | tf_op jit(solution)/shard_map/ppermute | solution.py:35
  22.8 2.3 %fusion.19 = f32[256,4096]{1,0:T(8,128)S(1)} fusion(bf16[1024,4096]{1,0:T(8,128)(2,1)S(1)} %bitcast.69, bf16[128,1024]{1,0:T(8,128)(2,1)S(1)} %get-tuple-element.72, bf16[128,1024]{1,0:T(8,128)(2,1)S(1)} %get-tuple-element.71), kind=kOutput, calls=%fused_computation.42 | convolution fusion | flops 2148532224 | bytes 13107200 | tf_op jit(solution)/shard_map/dot_general | solution.py:16
  25.1 4.1 %collective-permute-done.2 = bf16[32,4096]{1,0:T(8,128)(2,1)S(1)} collective-permute-done((bf16[32,4096]{1,0:T(8,128)(2,1)S(1)}, bf16[32,4096]{1,0:T(8,128)(2,1)S(1)}, u32[]{:S(2)}, u32[]{:S(2)}) %collective-permute-start.2) | collective-permute-done | bytes 262176 | tf_op jit(solution)/shard_map/ppermute | solution.py:35
  29.2 5.6 %collective-permute-done.4 = bf16[32,4096]{1,0:T(8,128)(2,1)S(1)} collective-permute-done((bf16[32,4096]{1,0:T(8,128)(2,1)S(1)}, bf16[32,4096]{1,0:T(8,128)(2,1)S(1)}, u32[]{:S(2)}, u32[]{:S(2)}) %collective-permute-start.4) | collective-permute-done | bytes 262176 | tf_op jit(solution)/shard_map/ppermute | solution.py:35
  35.5 1.9 %copy-done.1 = f32[256,4096]{1,0:T(8,128)} copy-done((f32[256,4096]{1,0:T(8,128)}, f32[256,4096]{1,0:T(8,128)S(1)}, u32[]{:S(2)}) %copy-start.1) | copy-done | bytes 4194328
  39.2 1.3 %collective-permute-start.6 = (bf16[32,4096]{1,0:T(8,128)(2,1)S(1)}, bf16[32,4096]{1,0:T(8,128)(2,1)S(1)}, u32[]{:S(2)}, u32[]{:S(2)}) collective-permute-start(bf16[32,4096]{1,0:T(8,128)(2,1)S(1)} %get-tuple-element.66), channel_id=1, source_target_pairs={{0,2},{1,3},{2,0},{3,1},{4,6},{5,7},{6,4},{7,5},{8,10},{9,11},{10,... | collective-permute-start | bytes 786440 | tf_op jit(solution)/shard_map/ppermute | solution.py:35
  42.3 2.4 %pad_maximum_fusion = bf16[512,4096]{1,0:T(8,128)(2,1)} fusion(bf16[256,4096]{1,0:T(8,128)(2,1)S(1)} %collective-permute-done.5, bf16[256,4096]{1,0:T(8,128)(2,1)S(1)} %bitcast.73), kind=kLoop, calls=%fused_computation.5 | loop fusion | flops 8388608 | bytes 8388608 | tf_op jit(solution)/shard_map/concatenate | solution.py:174
  46.7 1.3 collective-permute-start.11
  51.3 1.3 %collective-permute-start.8 = (f32[1,4096]{1,0:T(1,128)S(1)}, f32[1,4096]{1,0:T(1,128)S(1)}, u32[]{:S(2)}, u32[]{:S(2)}) collective-permute-start(f32[1,4096]{1,0:T(1,128)S(1)} %add.108), channel_id=1, source_target_pairs={{0,2},{1,3},{2,0},{3,1},{4,6},{5,7},{6,4},{7,5},{8,10},{9,11},{10,... | collective-permute-start | bytes 49160 | tf_op jit(solution)/shard_map/ppermute | solution.py:35
  53.0 4.8 %fusion.35 = f32[128,4096]{1,0:T(8,128)S(1)} fusion(bf16[1024,4096]{1,0:T(8,128)(2,1)} %get-tuple-element.31, bf16[1024,64]{0,1:T(8,128)(2,1)S(1)} %get-tuple-element.82, bf16[1024,64]{0,1:T(8,128)(2,1)S(1)} %get-tuple-element.81), kind=kOutput, calls=%fused_computation.75 | convolution fusion | flops 1074266112 | bytes 10747904 | tf_op jit(solution)/shard_map/dot_general | solution.py:16
  57.7 1.3 %collective-permute-start.9 = (bf16[32,4096]{1,0:T(8,128)(2,1)S(1)}, bf16[32,4096]{1,0:T(8,128)(2,1)S(1)}, u32[]{:S(2)}, u32[]{:S(2)}) collective-permute-start(bf16[32,4096]{1,0:T(8,128)(2,1)S(1)} %get-tuple-element.65), channel_id=1, source_target_pairs={{0,2},{1,3},{2,0},{3,1},{4,6},{5,7},{6,4},{7,5},{8,10},{9,11},{10,... | collective-permute-start | bytes 786440 | tf_op jit(solution)/shard_map/ppermute | solution.py:35
  61.6 3.6 %collective-permute-done.9 = bf16[32,4096]{1,0:T(8,128)(2,1)S(1)} collective-permute-done((bf16[32,4096]{1,0:T(8,128)(2,1)S(1)}, bf16[32,4096]{1,0:T(8,128)(2,1)S(1)}, u32[]{:S(2)}, u32[]{:S(2)}) %collective-permute-start.9) | collective-permute-done | bytes 262176 | tf_op jit(solution)/shard_map/ppermute | solution.py:35
  65.1 7.1 %convolution_convert_fusion.1 = bf16[512,1024]{1,0:T(8,128)(2,1)S(1)} fusion(bf16[512,4096]{1,0:T(8,128)(2,1)S(1)} %multiply_convert_fusion, bf16[1024,4096]{1,0:T(8,128)(2,1)} %get-tuple-element.31), kind=kOutput, calls=%fused_computation.22 | convolution fusion | flops 4295491584 | bytes 13631488 | tf_op jit(solution)/shard_map/dot_general | solution.py:16
  72.2 1.5 %fusion.11 = f32[128,512]{1,0:T(8,128)S(1)} fusion(bf16[512,4096]{1,0:T(8,128)(2,1)S(1)} %multiply_convert_fusion, bf16[64,4096]{1,0:T(8,128)(2,1)S(1)} %copy-done.5, bf16[64,4096]{1,0:T(8,128)(2,1)S(1)} %copy-done.7), kind=kOutput, calls=%fused_computation.31 | convolution fusion | flops 538968064 | bytes 5505024 | tf_op jit(solution)/shard_map/dot_general | solution.py:16
  77.8 2.9 %fusion.15 = f32[128,1024]{1,0:T(8,128)S(1)} fusion(bf16[1024,4096]{1,0:T(8,128)(2,1)S(1)} %bitcast.71, bf16[64,4096]{1,0:T(8,128)(2,1)S(1)} %get-tuple-element.58, bf16[64,4096]{1,0:T(8,128)(2,1)S(1)} %get-tuple-element.57), kind=kOutput, calls=%fused_computation.35 | convolution fusion | flops 1075838976 | bytes 9961472 | tf_op jit(solution)/shard_map/dot_general | solution.py:16
  82.0 12.0 %shard_map.110 = f32[80,1024]{1,0:T(8,128)S(1)} custom-call(bf16[4,80,1024]{2,1,0:T(8,128)(2,1)S(1)} %maximum_bitcast_fusion.x_ref), custom_call_target="tpu_custom_call" | custom-call | tf_op jit(solution)/shard_map/pallas_call | solution.py:112
  94.1 18.8 %shard_map.111 = f32[8,144,128]{2,1,0:T(8,128)S(1)} custom-call(bf16[8,144,128]{2,1,0:T(8,128)(2,1)S(1)} %maximum_bitcast_fusion.1.x_ref), custom_call_target="tpu_custom_call" | custom-call | tf_op jit(solution)/shard_map/pallas_call | solution.py:112
  113.7 10.7 %shard_map.112 = f32[4,80,1024]{2,1,0:T(8,128)S(1)} custom-call(bf16[80,1024]{1,0:T(8,128)(2,1)S(1)} %copy_bitcast_fusion.1.x_ref), custom_call_target="tpu_custom_call" | custom-call | tf_op jit(solution)/shard_map/pallas_call | solution.py:112
  126.3 1.3 multiply_convert_fusion.1
  (110 shorter events, 21.5 us)
Async XLA Ops:
  2.0 9.5 %collective-permute-start = (bf16[32,4096]{1,0:T(8,128)(2,1)S(1)}, bf16[32,4096]{1,0:T(8,128)(2,1)}, u32[]{:S(2)}, u32[]{:S(2)}) collective-permute-start(bf16[32,4096]{1,0:T(8,128)(2,1)S(1)} %get-tuple-element.69), channel_id=1, source_target_pairs={{0,2},{1,3},{2,0},{3,1},{4,6},{5,7},{6,4},{7,5},{8,10},{9,11},{10,... | collective-permute-start | bytes 786440 | tf_op jit(solution)/shard_map/ppermute | solution.py:35
  3.3 15.7 %collective-permute-start.1 = (bf16[32,4096]{1,0:T(8,128)(2,1)S(1)}, bf16[32,4096]{1,0:T(8,128)(2,1)}, u32[]{:S(2)}, u32[]{:S(2)}) collective-permute-start(bf16[32,4096]{1,0:T(8,128)(2,1)S(1)} %get-tuple-element.68), channel_id=1, source_target_pairs={{0,2},{1,3},{2,0},{3,1},{4,6},{5,7},{6,4},{7,5},{8,10},{9,11},{10,... | collective-permute-start | bytes 786440 | tf_op jit(solution)/shard_map/ppermute | solution.py:35
  11.5 27.1 %copy-start.8 = (bf16[128,1024]{1,0:T(8,128)(2,1)}, bf16[128,1024]{1,0:T(8,128)(2,1)S(1)}, u32[]{:S(2)}) copy-start(bf16[128,1024]{1,0:T(8,128)(2,1)S(1)} %get-tuple-element.71) | copy-start | bytes 786436
  11.5 27.1 %copy-start.10 = (bf16[128,1024]{1,0:T(8,128)(2,1)}, bf16[128,1024]{1,0:T(8,128)(2,1)S(1)}, u32[]{:S(2)}) copy-start(bf16[128,1024]{1,0:T(8,128)(2,1)S(1)} %get-tuple-element.72) | copy-start | bytes 786436
  11.5 27.1 %copy-start.12 = (bf16[128,1024]{1,0:T(8,128)(2,1)}, bf16[128,1024]{1,0:T(8,128)(2,1)S(1)}, u32[]{:S(2)}) copy-start(bf16[128,1024]{1,0:T(8,128)(2,1)S(1)} %get-tuple-element.73) | copy-start | bytes 786436
  11.5 27.1 %copy-start.14 = (bf16[128,1024]{1,0:T(8,128)(2,1)}, bf16[128,1024]{1,0:T(8,128)(2,1)S(1)}, u32[]{:S(2)}) copy-start(bf16[128,1024]{1,0:T(8,128)(2,1)S(1)} %get-tuple-element.74) | copy-start | bytes 786436
  11.6 11.2 %slice-start = ((s8[8388608]{0:T(1024)(128)(4,1)}), s8[4194304]{0:T(1024)(128)(4,1)S(1)}, s32[]{:S(2)}) async-start(s8[8388608]{0:T(1024)(128)(4,1)} %bitcast.68), calls=%async_computation | async-start | bytes 8388608
  12.9 9.8 %slice-start.1 = ((s8[8388608]{0:T(1024)(128)(4,1)}), s8[4194304]{0:T(1024)(128)(4,1)S(1)}, s32[]{:S(2)}) async-start(s8[8388608]{0:T(1024)(128)(4,1)} %bitcast.68), calls=%async_computation.1 | async-start | bytes 8388608
  20.0 14.8 %collective-permute-start.3 = (bf16[256,4096]{1,0:T(8,128)(2,1)S(1)}, bf16[256,4096]{1,0:T(8,128)(2,1)S(1)}, u32[]{:S(2)}, u32[]{:S(2)}) collective-permute-start(bf16[256,4096]{1,0:T(8,128)(2,1)S(1)} %convolution_convert_fusion), channel_id=1, source_target_pairs={{0,1},{1,0},{2,3},{3,2},{4,5},{5,4},{6,7},{7,6},{8,9},{9,8},{10,11... | collective-permute-start | bytes 6291464 | tf_op jit(solution)/shard_map/ppermute | solution.py:35
  21.3 7.9 %collective-permute-start.2 = (bf16[32,4096]{1,0:T(8,128)(2,1)S(1)}, bf16[32,4096]{1,0:T(8,128)(2,1)S(1)}, u32[]{:S(2)}, u32[]{:S(2)}) collective-permute-start(bf16[32,4096]{1,0:T(8,128)(2,1)S(1)} %get-tuple-element.70), channel_id=1, source_target_pairs={{0,2},{1,3},{2,0},{3,1},{4,6},{5,7},{6,4},{7,5},{8,10},{9,11},{10,... | collective-permute-start | bytes 786440 | tf_op jit(solution)/shard_map/ppermute | solution.py:35
  22.5 12.2 %collective-permute-start.4 = (bf16[32,4096]{1,0:T(8,128)(2,1)S(1)}, bf16[32,4096]{1,0:T(8,128)(2,1)S(1)}, u32[]{:S(2)}, u32[]{:S(2)}) collective-permute-start(bf16[32,4096]{1,0:T(8,128)(2,1)S(1)} %get-tuple-element.67), channel_id=1, source_target_pairs={{0,2},{1,3},{2,0},{3,1},{4,6},{5,7},{6,4},{7,5},{8,10},{9,11},{10,... | collective-permute-start | bytes 786440 | tf_op jit(solution)/shard_map/ppermute | solution.py:35
  37.6 4.7 %collective-permute-start.5 = (bf16[256,4096]{1,0:T(8,128)(2,1)S(1)}, bf16[256,4096]{1,0:T(8,128)(2,1)S(1)}, u32[]{:S(2)}, u32[]{:S(2)}) collective-permute-start(bf16[256,4096]{1,0:T(8,128)(2,1)S(1)} %bitcast.72), channel_id=1, source_target_pairs={{0,1},{1,0},{2,3},{3,2},{4,5},{5,4},{6,7},{7,6},{8,9},{9,8},{10,11... | collective-permute-start | bytes 6291464 | tf_op jit(solution)/shard_map/ppermute | solution.py:35
  38.5 12.8 %collective-permute-start.7 = (f32[1,4096]{1,0:T(1,128)S(1)}, f32[1,4096]{1,0:T(1,128)S(1)}, u32[]{:S(2)}, u32[]{:S(2)}) collective-permute-start(f32[1,4096]{1,0:T(1,128)S(1)} %bitcast.90), channel_id=1, source_target_pairs={{0,1},{1,0},{2,3},{3,2},{4,5},{5,4},{6,7},{7,6},{8,9},{9,8},{10,11... | collective-permute-start | bytes 49160 | tf_op jit(solution)/shard_map/ppermute | solution.py:35
  39.2 7.5 %collective-permute-start.6 = (bf16[32,4096]{1,0:T(8,128)(2,1)S(1)}, bf16[32,4096]{1,0:T(8,128)(2,1)S(1)}, u32[]{:S(2)}, u32[]{:S(2)}) collective-permute-start(bf16[32,4096]{1,0:T(8,128)(2,1)S(1)} %get-tuple-element.66), channel_id=1, source_target_pairs={{0,2},{1,3},{2,0},{3,1},{4,6},{5,7},{6,4},{7,5},{8,10},{9,11},{10,... | collective-permute-start | bytes 786440 | tf_op jit(solution)/shard_map/ppermute | solution.py:35
  46.7 5.9 %collective-permute-start.11 = (f32[1,4096]{1,0:T(1,128)S(1)}, f32[1,4096]{1,0:T(1,128)S(1)}, u32[]{:S(2)}, u32[]{:S(2)}) collective-permute-start(f32[1,4096]{1,0:T(1,128)S(1)} %bitcast.86), channel_id=1, source_target_pairs={{0,1},{1,0},{2,3},{3,2},{4,5},{5,4},{6,7},{7,6},{8,9},{9,8},{10,11... | collective-permute-start | bytes 49160 | tf_op jit(solution)/shard_map/ppermute | solution.py:35
  51.3 9.2 %collective-permute-start.8 = (f32[1,4096]{1,0:T(1,128)S(1)}, f32[1,4096]{1,0:T(1,128)S(1)}, u32[]{:S(2)}, u32[]{:S(2)}) collective-permute-start(f32[1,4096]{1,0:T(1,128)S(1)} %add.108), channel_id=1, source_target_pairs={{0,2},{1,3},{2,0},{3,1},{4,6},{5,7},{6,4},{7,5},{8,10},{9,11},{10,... | collective-permute-start | bytes 49160 | tf_op jit(solution)/shard_map/ppermute | solution.py:35
  52.7 7.9 %copy-start.17 = (f32[4096]{0:T(1024)S(1)}, f32[4096]{0:T(1024)}, u32[]{:S(2)}) copy-start(f32[4096]{0:T(1024)} %param.11) | copy-start | bytes 49156
  52.7 7.9 %collective-permute-start.12 = (f32[1,4096]{1,0:T(1,128)S(1)}, f32[1,4096]{1,0:T(1,128)S(1)}, u32[]{:S(2)}, u32[]{:S(2)}) collective-permute-start(f32[1,4096]{1,0:T(1,128)S(1)} %get-tuple-element.86), channel_id=1, source_target_pairs={{0,2},{1,3},{2,0},{3,1},{4,6},{5,7},{6,4},{7,5},{8,10},{9,11},{10,... | collective-permute-start | bytes 49160 | tf_op jit(solution)/shard_map/ppermute | solution.py:35
  53.0 7.7 %copy-start = (bf16[512,4096]{1,0:T(8,128)(2,1)S(1)}, bf16[512,4096]{1,0:T(8,128)(2,1)}, u32[]{:S(2)}) copy-start(bf16[512,4096]{1,0:T(8,128)(2,1)} %pad_maximum_fusion) | copy-start | bytes 12582916
  57.7 7.4 %collective-permute-start.9 = (bf16[32,4096]{1,0:T(8,128)(2,1)S(1)}, bf16[32,4096]{1,0:T(8,128)(2,1)S(1)}, u32[]{:S(2)}, u32[]{:S(2)}) collective-permute-start(bf16[32,4096]{1,0:T(8,128)(2,1)S(1)} %get-tuple-element.65), channel_id=1, source_target_pairs={{0,2},{1,3},{2,0},{3,1},{4,6},{5,7},{6,4},{7,5},{8,10},{9,11},{10,... | collective-permute-start | bytes 786440 | tf_op jit(solution)/shard_map/ppermute | solution.py:35
  59.1 13.2 %collective-permute-start.10 = (bf16[32,4096]{1,0:T(8,128)(2,1)S(1)}, bf16[32,4096]{1,0:T(8,128)(2,1)S(1)}, u32[]{:S(2)}, u32[]{:S(2)}) collective-permute-start(bf16[32,4096]{1,0:T(8,128)(2,1)S(1)} %get-tuple-element.64), channel_id=1, source_target_pairs={{0,2},{1,3},{2,0},{3,1},{4,6},{5,7},{6,4},{7,5},{8,10},{9,11},{10,... | collective-permute-start | bytes 786440 | tf_op jit(solution)/shard_map/ppermute | solution.py:35
  59.3 17.1 %collective-permute-start.13 = (bf16[32,4096]{1,0:T(8,128)(2,1)S(1)}, bf16[32,4096]{1,0:T(8,128)(2,1)S(1)}, u32[]{:S(2)}, u32[]{:S(2)}) collective-permute-start(bf16[32,4096]{1,0:T(8,128)(2,1)S(1)} %get-tuple-element.63), channel_id=1, source_target_pairs={{0,2},{1,3},{2,0},{3,1},{4,6},{5,7},{6,4},{7,5},{8,10},{9,11},{10,... | collective-permute-start | bytes 786440 | tf_op jit(solution)/shard_map/ppermute | solution.py:35
  61.5 10.7 %copy-start.5 = (bf16[64,4096]{1,0:T(8,128)(2,1)S(1)}, bf16[64,4096]{1,0:T(8,128)(2,1)}, u32[]{:S(2)}) copy-start(bf16[64,4096]{1,0:T(8,128)(2,1)} %copy-done.4) | copy-start | bytes 1572868
  61.5 10.7 %copy-start.7 = (bf16[64,4096]{1,0:T(8,128)(2,1)S(1)}, bf16[64,4096]{1,0:T(8,128)(2,1)}, u32[]{:S(2)}) copy-start(bf16[64,4096]{1,0:T(8,128)(2,1)} %copy-done.6) | copy-start | bytes 1572868
  (14 other events, 47.2 us)

commit v3 on v2

--- a/solution.py
+++ b/solution.py
@@ -131,12 +131,12 @@
     rows = cotangent.shape[0]
 
     quarter = rows // 4
-    quarters = []
-    for i in range(4):
-        part = cotangent[i * quarter : (i + 1) * quarter]
+    halves = []
+    for i in range(2):
+        part = cotangent[i * 2 * quarter : (i + 1) * 2 * quarter]
         for bit in reversed(bits[1:]):
             part = jnp.concatenate([part, swap(part, "tensor", tp, bit)], axis=0)
-        quarters.append(part)
+        halves.append(part)
 
     b_high, b_low = two_parts(adapter_in)
     a_high, a_low = two_parts(adapter_out)
@@ -147,40 +147,37 @@
         0,
     )
     merged = base_weight.astype(full) + lowrank
-    merged_low, quarters[0] = tie(merged.astype(low), quarters[0])
+    merged_low, halves[0] = tie(merged.astype(low), halves[0])
     square_sum = total(jnp.sum(merged * merged, axis=0)[None, :], "tensor", tp)
-    col_norm = jnp.sqrt(square_sum + epsilon)
-    col_scale = magnitude[None, :] / col_norm
 
     act = jnp.concatenate(
         [lax.dynamic_slice_in_dim(activations, (me ^ k) * rows, rows, 0) for k in order], axis=0
     )
     half = act.shape[0] // 2
     sent = mm(act[half:], merged_low, 1, 0).astype(low)
-    merged_low, sent, quarters[1] = tie(merged_low, sent, quarters[1])
+    merged_low, sent, halves[1] = tie(merged_low, sent, halves[1])
     kept = mm(act[:half], merged_low, 1, 0)
-    kept, quarters[2] = tie(kept, quarters[2])
     summed = kept + swap(sent, "tensor", tp, bits[0]).astype(full)
     for bit in bits[1:-1]:
         half = summed.shape[0] // 2
         summed = summed[:half] + swap(summed[half:].astype(low), "tensor", tp, bit).astype(full)
     passed, own = summed[rows:].astype(low), summed[:rows]
-    passed, own, quarters[3] = tie(passed, own, quarters[3])
-    arrived = [
-        swap(passed[i * quarter : (i + 1) * quarter], "tensor", tp, bits[-1]) for i in range(4)
-    ]
-    cot = jnp.concatenate([part.reshape(-1, quarter, part.shape[1]) for part in quarters], axis=1)
+    passed, own, square_sum = tie(passed, own, square_sum)
+    col_norm = jnp.sqrt(square_sum + epsilon)
+    col_scale = magnitude[None, :] / col_norm
+    arrived = [swap(part, "tensor", tp, bits[-1]) for part in (passed[:quarter], passed[quarter:])]
+    cot = jnp.concatenate([part.reshape(-1, 2 * quarter, part.shape[1]) for part in halves], axis=1)
     cot = cot.reshape(-1, cot.shape[2])
     cot = jnp.concatenate([cot, swap(cot, "tensor", tp, bits[0])], axis=0)
+    cot, arrived[0] = tie(cot, arrived[0])
     half = kept.shape[0]
     slope = (
         jnp.sum(cot[:half].astype(full) * kept, axis=0)
         + jnp.sum(cot[half:].astype(full) * sent.astype(full), axis=0)
     )[None, :]
-    slope, cot, arrived[0] = tie(slope, cot, arrived[0])
-    grad_scaled, arrived[1] = tie((cot.astype(full) * col_scale).astype(low), arrived[1])
+    grad_scaled = (cot.astype(full) * col_scale).astype(low)
     act_rel = mm(grad_scaled, merged_low, 1, 1).astype(low)
-    act_rel, grad_scaled, arrived[2] = tie(act_rel, grad_scaled, arrived[2])
+    act_rel, grad_scaled, arrived[1] = tie(act_rel, grad_scaled, arrived[1])
     places = jnp.asarray(place, jnp.int32)
     grad_act = jnp.concatenate(
         [lax.dynamic_slice_in_dim(act_rel, places[me ^ k] * rows, rows, 0) for k in range(tp)], axis=0
@@ -199,7 +196,6 @@
     slope_replica = total(slope, "tensor", tp)
     norm_coeff = -slope_replica * magnitude[None, :] / (col_norm * col_norm * col_norm)
     out_part = out_part + norm_coeff * own_dir
-    out_part, in_part, norm_coeff, arrived[3] = tie(out_part, in_part, norm_coeff, arrived[3])
     in_part = in_part + fold(
         mm(jnp.concatenate(two_parts(adapter_out * norm_coeff), axis=0), merged_low, 1, 1)
     )

time: 128 us -> 134 us (1.047)
  waiting for transfers between devices: 15.6 us -> 21.6 us
  other arithmetic: 11.9 us -> 15.3 us
  Pallas kernels: 41.4 us -> 39.4 us
  starting transfers between devices: 12.3 us -> 10.3 us
    ppermute x14 -> x10, waiting for transfers between devices: 15.6 us -> 21.6 us  [swap(): return lax.ppermute(x, axis, [(i, i ^ bit) for i in range(size)])]
    convert_element_type x1, other arithmetic: 0.88 us -> 3.21 us  [shards(): grad_scaled = (cot.astype(full) * col_scale).astype(low)]
    pallas_call x3, Pallas kernels: 41.4 us -> 39.4 us  [exchange(): pl.pallas_call(functools.partial(exchange_kernel, axis, size, scatter, ga...]
    unnamed x47 -> x57, local copies, waits for them, and re-layouts: 4.31 us -> 2.28 us
    concatenate x1, other arithmetic: 2.43 us -> 0.49 us  [shards(): cot = jnp.concatenate([cot, swap(cot, 'tensor', tp, bits[0])], axis=0)]
    ppermute x14 -> x10, starting transfers between devices: 12.3 us -> 10.3 us  [swap(): return lax.ppermute(x, axis, [(i, i ^ bit) for i in range(size)])]
  transfers between devices with their start and end apart: 14 -> 10, of which waited for: 5 -> 6; matrix products, arithmetic and copies ran while one was open for 30% -> 31% of each run, Pallas kernels for 0% -> 0%
where the time goes in v3:
time: 134 us
  Pallas kernels  39.4 us (29%)
  matrix products  34 us (25%)
  waiting for transfers between devices  21.6 us (16%)
  other arithmetic  15.3 us (11%)
  starting transfers between devices  10.3 us (8%)
  local copies, waits for them, and re-layouts  9.43 us (7%)
  between operations  3.89 us (3%)
    pallas_call x3, Pallas kernels, exchange(): pl.pallas_call(functools.partial(exchange_kernel, axis, size, scatter, ga...  39.4 us
    dot_general x10, matrix products, mm(): lax.dot_general(a, b, (((ca,), (cb,)), ((), ())), preferred_element_type=...  34 us
    ppermute x10, waiting for transfers between devices, swap(): return lax.ppermute(x, axis, [(i, i ^ bit) for i in range(size)])  21.6 us
    ppermute x10, starting transfers between devices, swap(): return lax.ppermute(x, axis, [(i, i ^ bit) for i in range(size)])  10.3 us
    convert_element_type x1, other arithmetic, shards(): grad_scaled = (cot.astype(full) * col_scale).astype(low)  3.21 us
  transfers between devices with their start and end apart: 10, of which 6 were waited for; matrix products, arithmetic and copies ran while one was open for 31% of the time, Pallas kernels for 0%

profile of v3, /device:TPU:25, one launch (start us, length us, event | category | flops | bytes accessed | tf_op | source)
XLA Modules:
  0.0 133.9 jit_solution(6577256267009940153)
XLA Ops:
  0.7 1.4 %fusion.59 = (bf16[64,4096]{1,0:T(8,128)(2,1)S(1)}, bf16[64,4096]{1,0:T(8,128)(2,1)S(1)}) fusion(bf16[128,4096]{1,0:T(8,128)(2,1)} %param.12), kind=kLoop, calls=%fused_computation.114 | loop fusion | bytes 2097152 | tf_op jit(solution)/shard_map/slice | solution.py:136
  2.0 1.3 collective-permute-start
  3.8 7.8 %multiply_reduce_fusion = (f32[4096]{0:T(1024)S(1)}, bf16[1024,4096]{1,0:T(8,128)(2,1)}) fusion(bf16[1024,4096]{1,0:T(8,128)(2,1)} %param.8, bf16[64,4096]{1,0:T(8,128)(2,1)S(1)} %get-tuple-element.56, bf16[64,4096]{1,0:T(8,128)(2,1)S(1)} %get-tuple-element.55, bf16[1024,64]{0,1:T(8,128)(2,1)S(1)} %get-tuple-element.62, bf16[1024,64]{0,1:T(8,128)(2,1)S(1)} %get-tuple-element.61), kind=kOutput, calls=%fused_computation | convolution fusion | flops 1637478400 | bytes 18104320 | tf_op jit(solution)/shard_map/dot_general | solution.py:16
  11.7 3.3 %collective-permute-done = bf16[64,4096]{1,0:T(8,128)(2,1)} collective-permute-done((bf16[64,4096]{1,0:T(8,128)(2,1)S(1)}, bf16[64,4096]{1,0:T(8,128)(2,1)}, u32[]{:S(2)}, u32[]{:S(2)}) %collective-permute-start) | collective-permute-done | bytes 524320 | tf_op jit(solution)/shard_map/ppermute | solution.py:35
  16.3 5.9 %convolution_convert_fusion = bf16[256,4096]{1,0:T(8,128)(2,1)S(1)} fusion(bf16[1024,4096]{1,0:T(8,128)(2,1)} %get-tuple-element.22, bf16[128,1024]{1,0:T(8,128)(2,1)S(1)} %get-tuple-element.51, bf16[128,1024]{1,0:T(8,128)(2,1)S(1)} %get-tuple-element.52), kind=kOutput, calls=%fused_computation.4 | convolution fusion | flops 2149580800 | bytes 11010048 | tf_op jit(solution)/shard_map/dot_general | solution.py:16
  22.2 4.1 %collective-permute-done.1 = bf16[64,4096]{1,0:T(8,128)(2,1)} collective-permute-done((bf16[64,4096]{1,0:T(8,128)(2,1)S(1)}, bf16[64,4096]{1,0:T(8,128)(2,1)}, u32[]{:S(2)}, u32[]{:S(2)}) %collective-permute-start.1) | collective-permute-done | bytes 524320 | tf_op jit(solution)/shard_map/ppermute | solution.py:35
  27.4 1.6 %collective-permute-start.2 = (bf16[256,4096]{1,0:T(8,128)(2,1)S(1)}, bf16[256,4096]{1,0:T(8,128)(2,1)S(1)}, u32[]{:S(2)}, u32[]{:S(2)}) collective-permute-start(bf16[256,4096]{1,0:T(8,128)(2,1)S(1)} %convolution_convert_fusion), channel_id=1, source_target_pairs={{0,1},{1,0},{2,3},{3,2},{4,5},{5,4},{6,7},{7,6},{8,9},{9,8},{10,11... | collective-permute-start | bytes 6291464 | tf_op jit(solution)/shard_map/ppermute | solution.py:35
  29.8 6.0 %collective-permute-done.3 = f32[1,4096]{1,0:T(1,128)S(1)} collective-permute-done((f32[1,4096]{1,0:T(1,128)S(1)}, f32[1,4096]{1,0:T(1,128)S(1)}, u32[]{:S(2)}, u32[]{:S(2)}) %collective-permute-start.3) | collective-permute-done | bytes 16416 | tf_op jit(solution)/shard_map/ppermute | solution.py:35
  35.8 1.3 collective-permute-start.4
  38.5 2.3 %fusion.19 = f32[256,4096]{1,0:T(8,128)S(1)} fusion(bf16[1024,4096]{1,0:T(8,128)(2,1)S(1)} %bitcast.64, bf16[128,1024]{1,0:T(8,128)(2,1)S(1)} %get-tuple-element.50, bf16[128,1024]{1,0:T(8,128)(2,1)S(1)} %get-tuple-element.49), kind=kOutput, calls=%fused_computation.44 | convolution fusion | flops 2148532224 | bytes 13107200 | tf_op jit(solution)/shard_map/dot_general | solution.py:16
  41.4 2.0 %copy-done.1 = f32[256,4096]{1,0:T(8,128)} copy-done((f32[256,4096]{1,0:T(8,128)}, f32[256,4096]{1,0:T(8,128)S(1)}, u32[]{:S(2)}) %copy-start.1) | copy-done | bytes 4194328
  43.6 1.3 collective-permute-start.6
  45.5 4.5 %collective-permute-done.6 = bf16[32,4096]{1,0:T(8,128)(2,1)S(1)} collective-permute-done((bf16[32,4096]{1,0:T(8,128)(2,1)S(1)}, bf16[32,4096]{1,0:T(8,128)(2,1)S(1)}, u32[]{:S(2)}, u32[]{:S(2)}) %collective-permute-start.6) | collective-permute-done | bytes 262176 | tf_op jit(solution)/shard_map/ppermute | solution.py:35
  51.8 2.4 %collective-permute-start.8 = (f32[1,4096]{1,0:T(1,128)S(1)}, f32[1,4096]{1,0:T(1,128)S(1)}, u32[]{:S(2)}, u32[]{:S(2)}) collective-permute-start(f32[1,4096]{1,0:T(1,128)S(1)} %bitcast.78), channel_id=1, source_target_pairs={{0,1},{1,0},{2,3},{3,2},{4,5},{5,4},{6,7},{7,6},{8,9},{9,8},{10,11... | collective-permute-start | bytes 49160 | tf_op jit(solution)/shard_map/ppermute | solution.py:35
  60.1 4.6 %fusion.35 = f32[128,4096]{1,0:T(8,128)S(1)} fusion(bf16[1024,4096]{1,0:T(8,128)(2,1)} %get-tuple-element.22, bf16[1024,64]{0,1:T(8,128)(2,1)S(1)} %get-tuple-element.62, bf16[1024,64]{0,1:T(8,128)(2,1)S(1)} %get-tuple-element.61), kind=kOutput, calls=%fused_computation.73 | convolution fusion | flops 1074266112 | bytes 10747904 | tf_op jit(solution)/shard_map/dot_general | solution.py:16
  68.1 3.2 %multiply_convert_fusion = bf16[512,4096]{1,0:T(8,128)(2,1)S(1)} fusion(bf16[512,4096]{1,0:T(8,128)(2,1)} %copy-done, f32[4096]{0:T(1024)S(1)} %bitcast.74), kind=kLoop, calls=%fused_computation.3 | loop fusion | flops 6291456 | bytes 8404992 | tf_op jit(solution)/shard_map/convert_element_type | solution.py:178
  71.4 7.4 %convolution_convert_fusion.1 = bf16[512,1024]{1,0:T(8,128)(2,1)S(1)} fusion(bf16[512,4096]{1,0:T(8,128)(2,1)S(1)} %multiply_convert_fusion, bf16[1024,4096]{1,0:T(8,128)(2,1)} %get-tuple-element.22), kind=kOutput, calls=%fused_computation.22 | convolution fusion | flops 4295491584 | bytes 13631488 | tf_op jit(solution)/shard_map/dot_general | solution.py:16
  79.0 2.9 %fusion.15 = f32[128,1024]{1,0:T(8,128)S(1)} fusion(bf16[1024,4096]{1,0:T(8,128)(2,1)S(1)} %bitcast.66, bf16[64,4096]{1,0:T(8,128)(2,1)S(1)} %get-tuple-element.44, bf16[64,4096]{1,0:T(8,128)(2,1)S(1)} %get-tuple-element.43), kind=kOutput, calls=%fused_computation.37 | convolution fusion | flops 1075838976 | bytes 9961472 | tf_op jit(solution)/shard_map/dot_general | solution.py:16
  82.0 2.9 %collective-permute-done.7 = bf16[96,4096]{1,0:T(8,128)(2,1)} collective-permute-done((bf16[96,4096]{1,0:T(8,128)(2,1)}, bf16[96,4096]{1,0:T(8,128)(2,1)}, u32[]{:S(2)}, u32[]{:S(2)}) %collective-permute-start.7) | collective-permute-done | bytes 786464 | tf_op jit(solution)/shard_map/ppermute | solution.py:35
  84.8 1.5 %fusion.11 = f32[128,512]{1,0:T(8,128)S(1)} fusion(bf16[512,4096]{1,0:T(8,128)(2,1)S(1)} %multiply_convert_fusion, bf16[64,4096]{1,0:T(8,128)(2,1)S(1)} %copy-done.7, bf16[64,4096]{1,0:T(8,128)(2,1)S(1)} %copy-done.9), kind=kOutput, calls=%fused_computation.33 | convolution fusion | flops 538968064 | bytes 5505024 | tf_op jit(solution)/shard_map/dot_general | solution.py:16
  89.3 10.6 %shard_map.110 = f32[80,1024]{1,0:T(8,128)S(1)} custom-call(bf16[4,80,1024]{2,1,0:T(8,128)(2,1)S(1)} %maximum_bitcast_fusion.x_ref), custom_call_target="tpu_custom_call" | custom-call | tf_op jit(solution)/shard_map/pallas_call | solution.py:112
  100.1 17.7 %shard_map.111 = f32[8,144,128]{2,1,0:T(8,128)S(1)} custom-call(bf16[8,144,128]{2,1,0:T(8,128)(2,1)S(1)} %maximum_bitcast_fusion.1.x_ref), custom_call_target="tpu_custom_call" | custom-call | tf_op jit(solution)/shard_map/pallas_call | solution.py:112
  117.8 11.0 %shard_map.112 = f32[4,80,1024]{2,1,0:T(8,128)S(1)} custom-call(bf16[80,1024]{1,0:T(8,128)(2,1)S(1)} %copy_bitcast_fusion.1.x_ref), custom_call_target="tpu_custom_call" | custom-call | tf_op jit(solution)/shard_map/pallas_call | solution.py:112
  131.5 2.4 %multiply_convert_fusion.1 = bf16[128,4096]{1,0:T(8,128)(2,1)} fusion(f32[128,4096]{1,0:T(8,128)S(1)} %slice-done.4, bf16[96,4096]{1,0:T(8,128)(2,1)} %collective-permute-done.7, bf16[32,4096]{1,0:T(8,128)(2,1)S(1)} %copy-done.19, f32[4096]{0:T(1024)S(1)} %bitcast.75), kind=kLoop, calls=%fused_computation.11 | loop fusion | flops 3670016 | bytes 4210688 | tf_op jit(solution)/shard_map/convert_element_type | solution.py:204
  (111 shorter events, 20.5 us)
Async XLA Ops:
  2.0 13.0 %collective-permute-start = (bf16[64,4096]{1,0:T(8,128)(2,1)S(1)}, bf16[64,4096]{1,0:T(8,128)(2,1)}, u32[]{:S(2)}, u32[]{:S(2)}) collective-permute-start(bf16[64,4096]{1,0:T(8,128)(2,1)S(1)} %get-tuple-element.54), channel_id=1, source_target_pairs={{0,2},{1,3},{2,0},{3,1},{4,6},{5,7},{6,4},{7,5},{8,10},{9,11},{10,... | collective-permute-start | bytes 1572872 | tf_op jit(solution)/shard_map/ppermute | solution.py:35
  3.3 22.9 %collective-permute-start.1 = (bf16[64,4096]{1,0:T(8,128)(2,1)S(1)}, bf16[64,4096]{1,0:T(8,128)(2,1)}, u32[]{:S(2)}, u32[]{:S(2)}) collective-permute-start(bf16[64,4096]{1,0:T(8,128)(2,1)S(1)} %get-tuple-element.53), channel_id=1, source_target_pairs={{0,2},{1,3},{2,0},{3,1},{4,6},{5,7},{6,4},{7,5},{8,10},{9,11},{10,... | collective-permute-start | bytes 1572872 | tf_op jit(solution)/shard_map/ppermute | solution.py:35
  3.8 7.8 %copy-start.6 = (bf16[64,4096]{1,0:T(8,128)(2,1)}, bf16[64,4096]{1,0:T(8,128)(2,1)S(1)}, u32[]{:S(2)}) copy-start(bf16[64,4096]{1,0:T(8,128)(2,1)S(1)} %get-tuple-element.55) | copy-start | bytes 1572868
  3.8 7.8 %copy-start.8 = (bf16[64,4096]{1,0:T(8,128)(2,1)}, bf16[64,4096]{1,0:T(8,128)(2,1)S(1)}, u32[]{:S(2)}) copy-start(bf16[64,4096]{1,0:T(8,128)(2,1)S(1)} %get-tuple-element.56) | copy-start | bytes 1572868
  3.8 7.8 %copy-start.5 = (bf16[512,1024]{1,0:T(8,128)(2,1)S(1)}, bf16[512,1024]{1,0:T(8,128)(2,1)}, u32[]{:S(2)}) copy-start(bf16[512,1024]{1,0:T(8,128)(2,1)} %param.7) | copy-start | bytes 3145732
  11.7 25.4 %copy-start.14 = (bf16[128,1024]{1,0:T(8,128)(2,1)}, bf16[128,1024]{1,0:T(8,128)(2,1)S(1)}, u32[]{:S(2)}) copy-start(bf16[128,1024]{1,0:T(8,128)(2,1)S(1)} %get-tuple-element.51) | copy-start | bytes 786436
  11.7 25.4 %copy-start.16 = (bf16[128,1024]{1,0:T(8,128)(2,1)}, bf16[128,1024]{1,0:T(8,128)(2,1)S(1)}, u32[]{:S(2)}) copy-start(bf16[128,1024]{1,0:T(8,128)(2,1)S(1)} %get-tuple-element.52) | copy-start | bytes 786436
  11.7 26.8 %copy-start.10 = (bf16[128,1024]{1,0:T(8,128)(2,1)}, bf16[128,1024]{1,0:T(8,128)(2,1)S(1)}, u32[]{:S(2)}) copy-start(bf16[128,1024]{1,0:T(8,128)(2,1)S(1)} %get-tuple-element.49) | copy-start | bytes 786436
  11.7 26.8 %copy-start.12 = (bf16[128,1024]{1,0:T(8,128)(2,1)}, bf16[128,1024]{1,0:T(8,128)(2,1)S(1)}, u32[]{:S(2)}) copy-start(bf16[128,1024]{1,0:T(8,128)(2,1)S(1)} %get-tuple-element.50) | copy-start | bytes 786436
  15.0 23.5 %slice-start = ((s8[8388608]{0:T(1024)(128)(4,1)}), s8[4194304]{0:T(1024)(128)(4,1)S(1)}, s32[]{:S(2)}) async-start(s8[8388608]{0:T(1024)(128)(4,1)} %bitcast.63), calls=%async_computation | async-start | bytes 8388608
  16.3 22.2 %slice-start.1 = ((s8[8388608]{0:T(1024)(128)(4,1)}), s8[4194304]{0:T(1024)(128)(4,1)S(1)}, s32[]{:S(2)}) async-start(s8[8388608]{0:T(1024)(128)(4,1)} %bitcast.63), calls=%async_computation.1 | async-start | bytes 8388608
  27.4 13.5 %collective-permute-start.2 = (bf16[256,4096]{1,0:T(8,128)(2,1)S(1)}, bf16[256,4096]{1,0:T(8,128)(2,1)S(1)}, u32[]{:S(2)}, u32[]{:S(2)}) collective-permute-start(bf16[256,4096]{1,0:T(8,128)(2,1)S(1)} %convolution_convert_fusion), channel_id=1, source_target_pairs={{0,1},{1,0},{2,3},{3,2},{4,5},{5,4},{6,7},{7,6},{8,9},{9,8},{10,11... | collective-permute-start | bytes 6291464 | tf_op jit(solution)/shard_map/ppermute | solution.py:35
  29.2 15.8 %collective-permute-start.5 = (bf16[256,4096]{1,0:T(8,128)(2,1)S(1)}, bf16[256,4096]{1,0:T(8,128)(2,1)S(1)}, u32[]{:S(2)}, u32[]{:S(2)}) collective-permute-start(bf16[256,4096]{1,0:T(8,128)(2,1)S(1)} %bitcast.67), channel_id=1, source_target_pairs={{0,1},{1,0},{2,3},{3,2},{4,5},{5,4},{6,7},{7,6},{8,9},{9,8},{10,11... | collective-permute-start | bytes 6291464 | tf_op jit(solution)/shard_map/ppermute | solution.py:35
  29.3 6.5 %collective-permute-start.3 = (f32[1,4096]{1,0:T(1,128)S(1)}, f32[1,4096]{1,0:T(1,128)S(1)}, u32[]{:S(2)}, u32[]{:S(2)}) collective-permute-start(f32[1,4096]{1,0:T(1,128)S(1)} %bitcast.81), channel_id=1, source_target_pairs={{0,1},{1,0},{2,3},{3,2},{4,5},{5,4},{6,7},{7,6},{8,9},{9,8},{10,11... | collective-permute-start | bytes 49160 | tf_op jit(solution)/shard_map/ppermute | solution.py:35
  35.8 2.7 %collective-permute-start.4 = (f32[1,4096]{1,0:T(1,128)S(1)}, f32[1,4096]{1,0:T(1,128)S(1)}, u32[]{:S(2)}, u32[]{:S(2)}) collective-permute-start(f32[1,4096]{1,0:T(1,128)S(1)} %add.114), channel_id=1, source_target_pairs={{0,2},{1,3},{2,0},{3,1},{4,6},{5,7},{6,4},{7,5},{8,10},{9,11},{10,... | collective-permute-start | bytes 49160 | tf_op jit(solution)/shard_map/ppermute | solution.py:35
  43.6 6.3 %collective-permute-start.6 = (bf16[32,4096]{1,0:T(8,128)(2,1)S(1)}, bf16[32,4096]{1,0:T(8,128)(2,1)S(1)}, u32[]{:S(2)}, u32[]{:S(2)}) collective-permute-start(bf16[32,4096]{1,0:T(8,128)(2,1)S(1)} %slice.92), channel_id=1, source_target_pairs={{0,2},{1,3},{2,0},{3,1},{4,6},{5,7},{6,4},{7,5},{8,10},{9,11},{10,... | collective-permute-start | bytes 786440 | tf_op jit(solution)/shard_map/ppermute | solution.py:35
  45.4 8.9 %copy-start.22 = (s32[4]{0:T(128)S(1)}, s32[4]{0:T(128)}, u32[]{:S(2)}) copy-start(s32[4]{0:T(128)} %constant.32.clone) | copy-start | bytes 52
  51.8 6.4 %collective-permute-start.8 = (f32[1,4096]{1,0:T(1,128)S(1)}, f32[1,4096]{1,0:T(1,128)S(1)}, u32[]{:S(2)}, u32[]{:S(2)}) collective-permute-start(f32[1,4096]{1,0:T(1,128)S(1)} %bitcast.78), channel_id=1, source_target_pairs={{0,1},{1,0},{2,3},{3,2},{4,5},{5,4},{6,7},{7,6},{8,9},{9,8},{10,11... | collective-permute-start | bytes 49160 | tf_op jit(solution)/shard_map/ppermute | solution.py:35
  58.8 5.9 %copy-start.4 = (bf16[128,4096]{1,0:T(8,128)(2,1)S(1)}, bf16[128,4096]{1,0:T(8,128)(2,1)}, u32[]{:S(2)}) copy-start(bf16[128,4096]{1,0:T(8,128)(2,1)} %copy-done.3) | copy-start | bytes 3145732
  58.8 8.4 %collective-permute-start.9 = (f32[1,4096]{1,0:T(1,128)}, f32[1,4096]{1,0:T(1,128)}, u32[]{:S(2)}, u32[]{:S(2)}) collective-permute-start(f32[1,4096]{1,0:T(1,128)} %add.123), channel_id=1, source_target_pairs={{0,2},{1,3},{2,0},{3,1},{4,6},{5,7},{6,4},{7,5},{8,10},{9,11},{10,... | collective-permute-start | bytes 49160 | tf_op jit(solution)/shard_map/ppermute | solution.py:35
  65.7 19.2 %collective-permute-start.7 = (bf16[96,4096]{1,0:T(8,128)(2,1)}, bf16[96,4096]{1,0:T(8,128)(2,1)}, u32[]{:S(2)}, u32[]{:S(2)}) collective-permute-start(bf16[96,4096]{1,0:T(8,128)(2,1)} %slice.93), channel_id=1, source_target_pairs={{0,2},{1,3},{2,0},{3,1},{4,6},{5,7},{6,4},{7,5},{8,10},{9,11},{10,... | collective-permute-start | bytes 2359304 | tf_op jit(solution)/shard_map/ppermute | solution.py:35
  68.1 10.9 %slice-start.2 = ((s8[8388608]{0:T(1024)(128)(4,1)}), s8[4194304]{0:T(1024)(128)(4,1)S(1)}, s32[]{:S(2)}) async-start(s8[8388608]{0:T(1024)(128)(4,1)} %bitcast.65), calls=%async_computation.2 | async-start | bytes 8388608
  71.4 7.6 %slice-start.3 = ((s8[8388608]{0:T(1024)(128)(4,1)}), s8[4194304]{0:T(1024)(128)(4,1)S(1)}, s32[]{:S(2)}) async-start(s8[8388608]{0:T(1024)(128)(4,1)} %bitcast.65), calls=%async_computation.3 | async-start | bytes 8388608
  79.0 5.8 %copy-start.7 = (bf16[64,4096]{1,0:T(8,128)(2,1)S(1)}, bf16[64,4096]{1,0:T(8,128)(2,1)}, u32[]{:S(2)}) copy-start(bf16[64,4096]{1,0:T(8,128)(2,1)} %copy-done.6) | copy-start | bytes 1572868
  (15 other events, 47.4 us)
